TPU v7x, 32 devices: a whole 2x2x4 slice. The times are simulated.
32 devices in a mesh: gx: 8 (over z, x), gy: 4 (over y, core).
Axes of the slice: x: 2, y: 2, z: 4, core: 2. Of those that a mesh axis runs over, the one named last changes fastest.
Arguments:
- field: float32 [32, 512, 512], P(None, 'gx', 'gy'), may hold values from -6 to 6
- conductivity: float32 [32, 512, 512], P(None, 'gx', 'gy'), may hold values from 0.2 to 1
- rate: float32 [32, 512, 512], P(None, 'gx', 'gy'), may hold values from 0.05 to 0.5
- patch_cell: int32 [8192], P(('gx', 'gy')), may hold values from 0 to 255
- trainer: int32 [8192, 1], P(('gx', 'gy')), may hold values from 0 to 31; in each aligned block of 256 rows (0 to 255, 256 to 511, ...) at most 16 rows name the same one
- res_slot: int32 [32768], P(('gx', 'gy')), may hold values from 0 to 2047
- reservoir: bfloat16 [65536, 2048], P(('gx', 'gy')), may hold values from -6 to 6
- weights: float32 [2, 1024, 1024], P(None, ('gx', 'gy')), may hold values from -0.1875 to 0.1875
- w_mom: float32 [2, 1024, 1024], P(None, ('gx', 'gy')), may hold values from -0.75 to 0.75
- w_var: float32 [2, 1024, 1024], P(None, ('gx', 'gy')), may hold values from 0.001 to 0.1
- biases: float32 [2, 1024], P(None, ('gx', 'gy')), may hold values from -6 to 6
- b_mom: float32 [2, 1024], P(None, ('gx', 'gy')), may hold values from -0.75 to 0.75
- b_var: float32 [2, 1024], P(None, ('gx', 'gy')), may hold values from 0.001 to 2
Outputs:
- new_field: float32 [32, 512, 512], P(None, 'gx', 'gy')
- new_weights: float32 [2, 1024, 1024], P(None, ('gx', 'gy'))
- new_w_mom: float32 [2, 1024, 1024], P(None, ('gx', 'gy'))
- new_w_var: float32 [2, 1024, 1024], P(None, ('gx', 'gy'))
- new_biases: float32 [2, 1024], P(None, ('gx', 'gy'))
- new_b_mom: float32 [2, 1024], P(None, ('gx', 'gy'))
- new_b_var: float32 [2, 1024], P(None, ('gx', 'gy'))
Inputs may be any that keep to these rules, and one draw needn't show every extreme that they name: At most 16 of the patches of one device go to one trainer. `res_slot`: slots of the trainer's own reservoir.
All inputs are finite; a program needn't handle non-finite values.
Results may differ from a plain program's by a relative error of at most 0.0003.
The roundings to bfloat16 on the way count: a program that leaves them out, or rounds other values in their place, can miss the bound.
Values may be sent and summed in bfloat16 or wider, within the bound.
A program may use at most 128 MiB of HBM per device.

v0:
```python
import jax
import jax.numpy as jnp
from jax import lax
from jax.sharding import PartitionSpec as P

PW = 32
STEPS = 4


time_step = 0.15
learn_rate = 0.001
beta_one = 0.9
beta_two = 0.99
adam_count = 20
tiny_eps = 1e-08


def with_halo(x, sides, width):
    for axis, dim in sides:
        peers, length = (lax.axis_size(axis), x.shape[dim])
        up = [(i, (i + 1) % peers) for i in range(peers - 1)]
        down = [(j, i) for i, j in up]
        last = lax.slice_in_dim(x, length - width, length, axis=dim)
        first = lax.slice_in_dim(x, 0, width, axis=dim)
        before = lax.ppermute(last, axis, up)
        after = lax.ppermute(first, axis, down)
        x = jnp.concatenate([before, x, after], axis=dim)
    return x


def update(padded, kpad, rate_inner):
    inner = slice(1, -1)
    centre = padded[1:-1, 1:-1, 1:-1]
    kcentre = kpad[1:-1, 1:-1, 1:-1]
    sides = [
        (slice(2, None), inner, inner),
        (slice(None, -2), inner, inner),
        (inner, slice(2, None), inner),
        (inner, slice(None, -2), inner),
        (inner, inner, slice(2, None)),
        (inner, inner, slice(None, -2)),
    ]
    flux = jnp.zeros_like(centre)
    for where in sides:
        flux = flux + 0.5 * (kcentre + kpad[where]) * (padded[where] - centre)
    return centre + time_step * (flux - rate_inner * centre)


def zpad(array):
    return jnp.pad(array, ((1, 1), (0, 0), (0, 0)))


def local_grads(rows, live, wbf, bbf):
    width = wbf.shape[1]
    inputs = rows[:, :width]
    target = rows[:, width:].astype(jnp.float32)
    pre = jnp.dot(inputs, wbf[0], preferred_element_type=jnp.float32) + bbf[0].astype(jnp.float32)
    hidden = jnp.tanh(pre)
    hidden_b = hidden.astype(jnp.bfloat16)
    pred = jnp.dot(hidden_b, wbf[1], preferred_element_type=jnp.float32) + bbf[1].astype(
        jnp.float32
    )
    count = jnp.sum(live)
    grad_pred = 2.0 * (pred - target) * live[:, None] / count
    grad_pred_b = grad_pred.astype(jnp.bfloat16)
    grad_w2 = jnp.dot(hidden_b.T, grad_pred_b, preferred_element_type=jnp.float32)
    grad_hid = jnp.dot(grad_pred_b, wbf[1].T, preferred_element_type=jnp.float32)
    grad_pre = grad_hid * (1.0 - hidden * hidden)
    grad_pre_b = grad_pre.astype(jnp.bfloat16)
    grad_w1 = jnp.dot(inputs.T, grad_pre_b, preferred_element_type=jnp.float32)
    return (jnp.stack([grad_w1, grad_w2]), jnp.stack([jnp.sum(grad_pre, 0), jnp.sum(grad_pred, 0)]))


def adam(param, moment, second, grad):
    moment_new = beta_one * moment + (1.0 - beta_one) * grad
    second_new = beta_two * second + (1.0 - beta_two) * grad * grad
    mhat = moment_new / (1.0 - beta_one**adam_count)
    vhat = second_new / (1.0 - beta_two**adam_count)
    return (param - learn_rate * mhat / (jnp.sqrt(vhat) + tiny_eps), moment_new, second_new)


def local(
    field,
    conductivity,
    rate,
    patch_cell,
    trainer,
    res_slot,
    reservoir,
    weights,
    w_mom,
    w_var,
    biases,
    b_mom,
    b_var,
):
    depth, cells_x, cells_y = field.shape
    state = field
    kpad = zpad(with_halo(conductivity, (("gx", 1), ("gy", 2)), 1))
    for step in range(STEPS):
        padded = with_halo(state, (("gx", 1), ("gy", 2)), 1)
        state = update(zpad(padded), kpad, rate)
    devices = lax.axis_size("gx") * lax.axis_size("gy")
    count_dev = patch_cell.shape[0]
    cap = max(2, 2 * count_dev // devices)
    stacked = jnp.stack([field, state]).reshape(2, depth, cells_x * cells_y // PW, PW)
    picked = stacked[:, :, patch_cell, :]
    patches = (
        jnp.transpose(picked, (2, 0, 1, 3)).reshape(count_dev, 2 * depth * PW).astype(jnp.bfloat16)
    )
    target_of = trainer[:, 0]
    onehot = (target_of[:, None] == jnp.arange(devices, dtype=jnp.int32)[None, :]).astype(jnp.int32)
    rank = jnp.sum(jnp.cumsum(onehot, 0) * onehot, 1) - 1
    where_to = target_of * cap + rank
    width2 = patches.shape[1]
    outbox = jnp.zeros((devices * cap, width2), jnp.bfloat16).at[where_to].set(patches)
    flags = (
        jnp.zeros((devices * cap,), jnp.bfloat16)
        .at[where_to]
        .set(jnp.ones((count_dev,), jnp.bfloat16))
    )
    arrived, alive = (
        lax.all_to_all(
            outbox.reshape(devices, cap, width2),
            ("gx", "gy"),
            split_axis=0,
            concat_axis=0,
            tiled=True,
        ),
        lax.all_to_all(
            flags.reshape(devices, cap), ("gx", "gy"), split_axis=0, concat_axis=0, tiled=True
        ),
    )
    arrived = arrived.reshape(devices * cap, width2)
    alive = alive.reshape(devices * cap).astype(jnp.float32)
    wfull, bfull = (
        lax.all_gather(weights.astype(jnp.bfloat16), ("gx", "gy"), axis=1, tiled=True),
        lax.all_gather(biases.astype(jnp.bfloat16), ("gx", "gy"), axis=1, tiled=True),
    )
    rows = jnp.concatenate([reservoir[res_slot], arrived], 0)
    live = jnp.concatenate([jnp.ones((res_slot.shape[0],), jnp.float32), alive])
    grad_w, grad_b = local_grads(rows, live, wfull, bfull)
    whole_w, whole_b = lax.psum((grad_w, grad_b), ("gx", "gy"))
    position = lax.axis_index("gx") * lax.axis_size("gy") + lax.axis_index("gy")
    share_w = lax.dynamic_slice_in_dim(whole_w, position * weights.shape[1], weights.shape[1], 1)
    share_b = lax.dynamic_slice_in_dim(whole_b, position * biases.shape[1], biases.shape[1], 1)
    new_w, new_wm, new_wv = adam(weights, w_mom, w_var, share_w)
    new_b, new_bm, new_bv = adam(biases, b_mom, b_var, share_b)
    return (state, new_w, new_wm, new_wv, new_b, new_bm, new_bv)


def solution(mesh):
    return jax.shard_map(
        local,
        mesh=mesh,
        in_specs=(
            P(None, "gx", "gy"),
            P(None, "gx", "gy"),
            P(None, "gx", "gy"),
            P(("gx", "gy")),
            P(("gx", "gy"), None),
            P(("gx", "gy")),
            P(("gx", "gy"), None),
            P(None, ("gx", "gy"), None),
            P(None, ("gx", "gy"), None),
            P(None, ("gx", "gy"), None),
            P(None, ("gx", "gy")),
            P(None, ("gx", "gy")),
            P(None, ("gx", "gy")),
        ),
        out_specs=(
            P(None, "gx", "gy"),
            P(None, ("gx", "gy"), None),
            P(None, ("gx", "gy"), None),
            P(None, ("gx", "gy"), None),
            P(None, ("gx", "gy")),
            P(None, ("gx", "gy")),
            P(None, ("gx", "gy")),
        ),
        check_vma=False,
    )
```

profile of v0, /device:TPU:0, one launch (start us, length us, event | category | flops | bytes accessed | tf_op | source)
XLA Modules:
  0.0 527.2 jit_solution(12032356917368722524)
XLA Ops:
  8.2 4.8 collective-permute-start
  15.4 4.5 collective-permute-start.4
  21.2 1.6 convert_element_type.50
  32.2 5.4 %collective-permute-start.6 = (f32[32,66,1]{1,0,2:T(8,128)}, f32[32,66,1]{1,0,2:T(8,128)}, u32[]{:S(2)}, u32[]{:S(2)}) collective-permute-start(f32[32,66,1]{1,0,2:T(8,128)} %copy.208), channel_id=1, source_target_pairs={{0,1},{1,2},{2,3},{4,5},{5,6},{6,7},{8,9},{9,10},{10,11},{12,13},{... | collective-permute-start | bytes 25352 | tf_op jit(solution)/shard_map/ppermute | solution.py:25
  39.9 1.5 copy.202
  41.5 1.5 copy.203
  43.0 2.8 select_maximum_fusion.16
  45.8 2.3 copy.210
  48.0 2.2 copy.211
  50.3 3.3 select_maximum_fusion.12
  54.0 5.1 fusion.70
  62.0 6.1 %collective-permute-start.8 = (f32[32,1,128]{2,0,1:T(8,128)}, f32[32,1,128]{2,0,1:T(8,128)}, u32[]{:S(2)}, u32[]{:S(2)}) collective-permute-start(f32[32,1,128]{2,0,1:T(8,128)} %bitcast.8), channel_id=1, source_target_pairs={{0,4},{4,8},{8,12},{12,16},{16,20},{20,24},{24,28},{1,5},{5,9},{9,... | collective-permute-start | bytes 49160 | tf_op jit(solution)/shard_map/ppermute | solution.py:25
  72.7 1.8 fusion.111
  74.5 2.3 copy.224
  76.9 4.0 collective-permute-start.10
  80.9 2.3 copy.225
  83.2 1.5 collective-permute-start.11
  84.7 1.4 fusion.99
  86.1 2.3 copy.226
  88.3 2.2 copy.227
  90.6 3.2 select_maximum_fusion.8
  94.2 5.1 fusion.52
  99.4 4.2 collective-permute-start.12
  105.5 3.8 collective-permute-done.13
  110.0 1.8 fusion.110
  111.8 2.3 copy.236
  114.2 3.5 collective-permute-start.14
  117.6 2.3 copy.237
  123.0 2.8 scatter_custom_fusion.1
  127.2 10.0 %all-to-all-start.1 = ((bf16[32,1,16]{2,1,0:T(2,128)(2,1)}), bf16[32,1,16]{2,1,0:T(2,128)(2,1)}, u32[]{:S(2)}, u32[]{:S(2)}) async-start(bf16[32,1,16]{2,1,0:T(2,128)(2,1)} %all_to_all.12), calls=%async_computation.1 | async-start | bytes 32768 | tf_op jit(solution)/shard_map/all_to_all | solution.py:130
  137.2 2.3 copy.238
  139.5 2.2 copy.239
  141.8 3.2 select_maximum_fusion.4
  145.4 5.1 fusion.34
  150.5 3.6 collective-permute-start.16
  156.0 3.8 collective-permute-done.17
  159.9 1.8 fusion.109
  161.7 2.3 copy.248
  164.0 1.9 collective-permute-start.18
  165.9 2.3 copy.249
  168.2 1.7 collective-permute-start.19
  171.1 3.7 stack.27
  174.9 4.3 copy.257
  179.2 2.3 copy.250
  181.4 2.3 copy.251
  183.8 3.2 select_maximum_fusion
  187.4 5.8 %fusion.16 = f32[32,64,128]{2,1,0:T(8,128)} fusion(f32[32,64,128]{2,1,0:T(8,128)S(1)} %copy-done.14, f32[32,66,1]{2,1,0:T(8,128)S(1)} %copy-done.21, f32[32,1,128]{2,1,0:T(1,128)S(1)} %bitcast.114, f32[32,1,128]{2,1,0:T(1,128)S(1)} %bitcast.111, f32[32,66,1]{2,1,0:T(8,128)} %copy.251, f32[34,66,130]{2,1,0:T(8,128)S(1)} %select_maximum_fusion, ...), kind=kLoop, calls=%fused_computation.57 | loop fusion | flops 12845056 | bytes 8487936 | tf_op jit(solution)/shard_map/add | solution.py:46
  193.2 2.7 stack.28
  197.5 3.0 pad_maximum_fusion
  200.5 5.5 %gather_fusion.1 = bf16[256,2,32,32]{3,2,1,0:T(8,128)(2,1)} fusion(bf16[2,32,256,32]{3,1,2,0:T(8,128)(2,1)} %pad_maximum_fusion, s32[1024]{0:T(1024)} %pad_clamp_fusion), kind=kCustom, calls=%fused_computation.1 | custom fusion | bytes 2098176 | tf_op jit(solution)/shard_map/gather | solution.py:107
  205.9 4.9 copy.259
  211.5 3.8 scatter_custom_fusion
  215.3 7.9 %all-to-all-start = ((bf16[32,16,2048]{2,1,0:T(8,128)(2,1)}), bf16[32,16,2048]{2,1,0:T(8,128)(2,1)S(1)}, u32[]{:S(2)}, u32[]{:S(2)}) async-start(bf16[32,16,2048]{2,1,0:T(8,128)(2,1)} %bitcast.32), calls=%async_computation | async-start | bytes 4194304 | tf_op jit(solution)/shard_map/all_to_all | solution.py:123
  223.3 69.0 %all-gather = bf16[32,32,2]{1,2,0:T(2,128)(2,1)S(1)} all-gather(bf16[1,32,2]{1,2,0:T(2,128)(2,1)S(1)} %convert_bitcast_fusion), channel_id=1, replica_groups=mesh['gx'=8,'gy'=4] {'gx','gy'}, dimensions={0}, use_global_device_ids=true | all-gather | bytes 4224 | tf_op jit(solution)/shard_map/all_gather | solution.py:138
  292.4 13.5 %gather_fusion = bf16[1024,2048]{1,0:T(8,128)(2,1)} fusion(bf16[2048,2048]{1,0:T(8,128)(2,1)} %param.19, s32[1024]{0:T(1024)S(1)} %fusion.101), kind=kCustom, calls=%fused_computation | custom fusion | bytes 8392704 | tf_op jit(solution)/shard_map/gather | solution.py:140
  307.4 5.9 %fusion.8 = f32[1536,1024]{1,0:T(8,128)S(1)} fusion(bf16[2,1024,1024]{2,1,0:T(8,128)(2,1)} %all-gather.3.cloned.1.call-done, bf16[1024,2048]{1,0:T(8,128)(2,1)} %gather_fusion, bf16[512,2048]{1,0:T(8,128)(2,1)S(1)} %bitcast.82), kind=kOutput, calls=%fused_computation.43 | convolution fusion | flops 3227516928 | bytes 14680064 | tf_op jit(solution)/shard_map/dot_general | solution.py:57
  313.3 6.1 %fusion.119 = (f32[1024]{0:T(1024)S(1)}, bf16[1536,1024]{1,0:T(8,128)(2,1)S(1)}) fusion(f32[]{:T(128)} %get-tuple-element.57, f32[1536]{0:T(1024)S(1)} %get-tuple-element.56, bf16[512,2048]{1,0:T(8,128)(2,1)S(1)} %bitcast.83, bf16[1024,2048]{1,0:T(8,128)(2,1)S(1)} %copy-done.26, f32[1024]{0:T(1024)S(1)} %bitcast.132, ...), kind=kOutput, calls=%fused_computation.225 | convolution fusion | flops 3240098816 | bytes 17846276 | tf_op jit(solution)/shard_map/dot_general | solution.py:60
  319.4 3.5 convolution_bitcast_fusion
  322.9 5.0 fusion.120
  327.9 3.6 fusion.5
  331.5 4.1 pad_maximum_fusion.1
  335.7 45.4 %psum.15 = f32[2,1024]{1,0:T(2,128)S(1)} all-reduce(f32[2,1024]{1,0:T(2,128)S(1)} %pad_maximum_fusion.48), channel_id=1, replica_groups=mesh['gx'=8,'gy'=4] {'gx','gy'}, use_global_device_ids=true, to_apply=%region_9.10 | all-reduce | flops 2048 | bytes 16384 | tf_op jit(solution)/shard_map/psum | solution.py:143
  381.8 136.4 %all-reduce.8.cloned.1.call-done = f32[2,1024,1024]{2,1,0:T(8,128)} async-done(((f32[2,1024,1024]{2,1,0:T(8,128)}), f32[2,1024,1024]{2,1,0:T(8,128)}) %all-reduce.8.cloned.1.call-update) | async-done | bytes 8388624 | tf_op jit(solution)/shard_map/psum | solution.py:143
  518.3 1.9 divide_subtract_fusion
  (193 shorter events, 40.2 us)
Async XLA Ops:
  7.2 300.2 %all-gather.3.cloned.1.call-start = ((), (), s32[]{:S(2)}) async-start(), calls=%async_computation.2 | async-start | bytes 4325376 | tf_op jit(solution)/shard_map/all_gather | solution.py:137
  8.2 16.5 %collective-permute-start = (f32[32,1,128]{2,0,1:T(8,128)S(1)}, f32[32,1,128]{2,0,1:T(8,128)S(1)}, u32[]{:S(2)}, u32[]{:S(2)}) collective-permute-start(f32[32,1,128]{2,0,1:T(8,128)S(1)} %bitcast.119), channel_id=1, source_target_pairs={{0,4},{4,8},{8,12},{12,16},{16,20},{20,24},{24,28},{1,5},{5,9},{9,... | collective-permute-start | bytes 49160 | tf_op jit(solution)/shard_map/ppermute | solution.py:25
  13.1 11.7 %collective-permute-start.1 = (f32[32,1,128]{2,0,1:T(8,128)S(1)}, f32[32,1,128]{2,0,1:T(8,128)S(1)}, u32[]{:S(2)}, u32[]{:S(2)}) collective-permute-start(f32[32,1,128]{2,0,1:T(8,128)S(1)} %bitcast.118), channel_id=1, source_target_pairs={{4,0},{8,4},{12,8},{16,12},{20,16},{24,20},{28,24},{5,1},{9,5},{13... | collective-permute-start | bytes 49160 | tf_op jit(solution)/shard_map/ppermute | solution.py:26
  15.4 15.2 %collective-permute-start.4 = (f32[32,1,128]{2,0,1:T(8,128)S(1)}, f32[32,1,128]{2,0,1:T(8,128)S(1)}, u32[]{:S(2)}, u32[]{:S(2)}) collective-permute-start(f32[32,1,128]{2,0,1:T(8,128)S(1)} %bitcast.117), channel_id=1, source_target_pairs={{0,4},{4,8},{8,12},{12,16},{16,20},{20,24},{24,28},{1,5},{5,9},{9,... | collective-permute-start | bytes 49160 | tf_op jit(solution)/shard_map/ppermute | solution.py:25
  19.9 10.7 %collective-permute-start.5 = (f32[32,1,128]{2,0,1:T(8,128)S(1)}, f32[32,1,128]{2,0,1:T(8,128)S(1)}, u32[]{:S(2)}, u32[]{:S(2)}) collective-permute-start(f32[32,1,128]{2,0,1:T(8,128)S(1)} %bitcast.116), channel_id=1, source_target_pairs={{4,0},{8,4},{12,8},{16,12},{20,16},{24,20},{28,24},{5,1},{9,5},{13... | collective-permute-start | bytes 49160 | tf_op jit(solution)/shard_map/ppermute | solution.py:26
  26.7 3.9 copy-start.9
  27.5 12.4 %collective-permute-start.2 = (f32[32,66,1]{1,0,2:T(8,128)S(1)}, f32[32,66,1]{1,0,2:T(8,128)S(1)}, u32[]{:S(2)}, u32[]{:S(2)}) collective-permute-start(f32[32,66,1]{1,0,2:T(8,128)S(1)} %copy.200), channel_id=1, source_target_pairs={{0,1},{1,2},{2,3},{4,5},{5,6},{6,7},{8,9},{9,10},{10,11},{12,13},{... | collective-permute-start | bytes 25352 | tf_op jit(solution)/shard_map/ppermute | solution.py:25
  29.3 12.2 %collective-permute-start.3 = (f32[32,66,1]{1,0,2:T(8,128)S(1)}, f32[32,66,1]{1,0,2:T(8,128)S(1)}, u32[]{:S(2)}, u32[]{:S(2)}) collective-permute-start(f32[32,66,1]{1,0,2:T(8,128)S(1)} %copy.201), channel_id=1, source_target_pairs={{1,0},{2,1},{3,2},{5,4},{6,5},{7,6},{9,8},{10,9},{11,10},{13,12},{... | collective-permute-start | bytes 25352 | tf_op jit(solution)/shard_map/ppermute | solution.py:26
  31.2 11.8 %copy-start.8 = (f32[32,64,128]{2,1,0:T(8,128)S(1)}, f32[32,64,128]{2,1,0:T(8,128)}, u32[]{:S(2)}) copy-start(f32[32,64,128]{2,1,0:T(8,128)} %param.14) | copy-start | bytes 3145732
  32.2 13.5 %collective-permute-start.6 = (f32[32,66,1]{1,0,2:T(8,128)}, f32[32,66,1]{1,0,2:T(8,128)}, u32[]{:S(2)}, u32[]{:S(2)}) collective-permute-start(f32[32,66,1]{1,0,2:T(8,128)} %copy.208), channel_id=1, source_target_pairs={{0,1},{1,2},{2,3},{4,5},{5,6},{6,7},{8,9},{9,10},{10,11},{12,13},{... | collective-permute-start | bytes 25352 | tf_op jit(solution)/shard_map/ppermute | solution.py:25
  38.6 9.4 %collective-permute-start.7 = (f32[32,66,1]{1,0,2:T(8,128)}, f32[32,66,1]{1,0,2:T(8,128)}, u32[]{:S(2)}, u32[]{:S(2)}) collective-permute-start(f32[32,66,1]{1,0,2:T(8,128)} %copy.209), channel_id=1, source_target_pairs={{1,0},{2,1},{3,2},{5,4},{6,5},{7,6},{9,8},{10,9},{11,10},{13,12},{... | collective-permute-start | bytes 25352 | tf_op jit(solution)/shard_map/ppermute | solution.py:26
  50.2 3.4 copy-start
  50.2 3.4 copy-start.4
  50.2 3.4 copy-start.10
  50.2 3.4 copy-start.17
  50.3 3.8 copy-start.24
  50.3 3.7 copy-start.29
  50.3 3.7 copy-start.34
  50.3 3.7 copy-start.42
  50.3 3.7 copy-start.44
  54.0 14.1 %copy-start.38 = (s32[32,2,128]{2,0,1:T(8,128)S(1)}, s32[32,2,128]{2,0,1:T(8,128)}, u32[]{:S(2)}) copy-start(s32[32,2,128]{2,0,1:T(8,128)} %reduce-window.6) | copy-start | bytes 98308
  60.7 10.7 %collective-permute-start.9 = (f32[32,1,128]{2,0,1:T(8,128)}, f32[32,1,128]{2,0,1:T(8,128)}, u32[]{:S(2)}, u32[]{:S(2)}) collective-permute-start(f32[32,1,128]{2,0,1:T(8,128)} %bitcast.10), channel_id=1, source_target_pairs={{4,0},{8,4},{12,8},{16,12},{20,16},{24,20},{28,24},{5,1},{9,5},{13... | collective-permute-start | bytes 49160 | tf_op jit(solution)/shard_map/ppermute | solution.py:26
  62.0 9.4 %collective-permute-start.8 = (f32[32,1,128]{2,0,1:T(8,128)}, f32[32,1,128]{2,0,1:T(8,128)}, u32[]{:S(2)}, u32[]{:S(2)}) collective-permute-start(f32[32,1,128]{2,0,1:T(8,128)} %bitcast.8), channel_id=1, source_target_pairs={{0,4},{4,8},{8,12},{12,16},{16,20},{20,24},{24,28},{1,5},{5,9},{9,... | collective-permute-start | bytes 49160 | tf_op jit(solution)/shard_map/ppermute | solution.py:25
  76.9 9.2 %collective-permute-start.10 = (f32[32,66,1]{1,0,2:T(8,128)}, f32[32,66,1]{1,0,2:T(8,128)}, u32[]{:S(2)}, u32[]{:S(2)}) collective-permute-start(f32[32,66,1]{1,0,2:T(8,128)} %copy.224), channel_id=1, source_target_pairs={{0,1},{1,2},{2,3},{4,5},{5,6},{6,7},{8,9},{9,10},{10,11},{12,13},{... | collective-permute-start | bytes 25352 | tf_op jit(solution)/shard_map/ppermute | solution.py:25
  83.2 5.1 collective-permute-start.11
  90.6 3.6 copy-start.22
  90.6 3.6 copy-start.30
  90.6 3.6 copy-start.35
  94.2 10.7 %copy-start.53 = (s32[256]{0:T(256)S(1)}, s32[256]{0:T(256)}, u32[]{:S(2)}) copy-start(s32[256]{0:T(256)} %fusion.99) | copy-start | bytes 3076
  99.4 12.5 %copy-start.11 = (f32[32,64,128]{2,1,0:T(8,128)}, f32[32,64,128]{2,1,0:T(8,128)S(1)}, u32[]{:S(2)}) copy-start(f32[32,64,128]{2,1,0:T(8,128)S(1)} %fusion.52) | copy-start | bytes 3145732
  99.4 6.1 %collective-permute-start.12 = (f32[32,1,128]{2,0,1:T(8,128)S(1)}, f32[32,1,128]{2,0,1:T(8,128)S(1)}, u32[]{:S(2)}, u32[]{:S(2)}) collective-permute-start(f32[32,1,128]{2,0,1:T(8,128)S(1)} %bitcast.122), channel_id=1, source_target_pairs={{0,4},{4,8},{8,12},{12,16},{16,20},{20,24},{24,28},{1,5},{5,9},{9,... | collective-permute-start | bytes 49160 | tf_op jit(solution)/shard_map/ppermute | solution.py:25
  103.7 5.6 %collective-permute-start.13 = (f32[32,1,128]{2,0,1:T(8,128)S(1)}, f32[32,1,128]{2,0,1:T(8,128)S(1)}, u32[]{:S(2)}, u32[]{:S(2)}) collective-permute-start(f32[32,1,128]{2,0,1:T(8,128)S(1)} %bitcast.120), channel_id=1, source_target_pairs={{4,0},{8,4},{12,8},{16,12},{20,16},{24,20},{28,24},{5,1},{9,5},{13... | collective-permute-start | bytes 49160 | tf_op jit(solution)/shard_map/ppermute | solution.py:26
  105.5 3.8 copy-start.45
  114.2 23.0 %collective-permute-start.14 = (f32[32,66,1]{1,0,2:T(8,128)}, f32[32,66,1]{1,0,2:T(8,128)}, u32[]{:S(2)}, u32[]{:S(2)}) collective-permute-start(f32[32,66,1]{1,0,2:T(8,128)} %copy.236), channel_id=1, source_target_pairs={{0,1},{1,2},{2,3},{4,5},{5,6},{6,7},{8,9},{9,10},{10,11},{12,13},{... | collective-permute-start | bytes 25352 | tf_op jit(solution)/shard_map/ppermute | solution.py:25
  119.9 19.5 %collective-permute-start.15 = (f32[32,66,1]{1,0,2:T(8,128)}, f32[32,66,1]{1,0,2:T(8,128)}, u32[]{:S(2)}, u32[]{:S(2)}) collective-permute-start(f32[32,66,1]{1,0,2:T(8,128)} %copy.237), channel_id=1, source_target_pairs={{1,0},{2,1},{3,2},{5,4},{6,5},{7,6},{9,8},{10,9},{11,10},{13,12},{... | collective-permute-start | bytes 25352 | tf_op jit(solution)/shard_map/ppermute | solution.py:26
  127.2 88.1 %all-to-all-start.1 = ((bf16[32,1,16]{2,1,0:T(2,128)(2,1)}), bf16[32,1,16]{2,1,0:T(2,128)(2,1)}, u32[]{:S(2)}, u32[]{:S(2)}) async-start(bf16[32,1,16]{2,1,0:T(2,128)(2,1)} %all_to_all.12), calls=%async_computation.1 | async-start | bytes 32768 | tf_op jit(solution)/shard_map/all_to_all | solution.py:130
  141.7 3.6 copy-start.23
  141.7 3.6 copy-start.31
  141.7 3.6 copy-start.36
  141.7 3.6 copy-start.46
  141.7 3.6 copy-start.48
  145.4 10.0 %copy-start.58 = (s32[256]{0:T(256)S(1)}, s32[256]{0:T(256)}, u32[]{:S(2)}) copy-start(s32[256]{0:T(256)} %param.16) | copy-start | bytes 3076
  150.4 11.2 %copy-start.13 = (f32[32,64,128]{2,1,0:T(8,128)}, f32[32,64,128]{2,1,0:T(8,128)S(1)}, u32[]{:S(2)}) copy-start(f32[32,64,128]{2,1,0:T(8,128)S(1)} %fusion.34) | copy-start | bytes 3145732
  150.5 5.5 %collective-permute-start.16 = (f32[32,1,128]{2,0,1:T(8,128)S(1)}, f32[32,1,128]{2,0,1:T(8,128)S(1)}, u32[]{:S(2)}, u32[]{:S(2)}) collective-permute-start(f32[32,1,128]{2,0,1:T(8,128)S(1)} %bitcast.123), channel_id=1, source_target_pairs={{0,4},{4,8},{8,12},{12,16},{16,20},{20,24},{24,28},{1,5},{5,9},{9,... | collective-permute-start | bytes 49160 | tf_op jit(solution)/shard_map/ppermute | solution.py:25
  154.1 5.6 %collective-permute-start.17 = (f32[32,1,128]{2,0,1:T(8,128)S(1)}, f32[32,1,128]{2,0,1:T(8,128)S(1)}, u32[]{:S(2)}, u32[]{:S(2)}) collective-permute-start(f32[32,1,128]{2,0,1:T(8,128)S(1)} %bitcast.121), channel_id=1, source_target_pairs={{4,0},{8,4},{12,8},{16,12},{20,16},{24,20},{28,24},{5,1},{9,5},{13... | collective-permute-start | bytes 49160 | tf_op jit(solution)/shard_map/ppermute | solution.py:26
  156.0 5.7 %copy-start.49 = (f32[32,1,128]{2,0,1:T(8,128)}, f32[32,1,128]{2,0,1:T(8,128)S(1)}, u32[]{:S(2)}) copy-start(f32[32,1,128]{2,0,1:T(8,128)S(1)} %collective-permute-done.16) | copy-start | bytes 49156
  164.0 15.2 %collective-permute-start.18 = (f32[32,66,1]{1,0,2:T(8,128)}, f32[32,66,1]{1,0,2:T(8,128)}, u32[]{:S(2)}, u32[]{:S(2)}) collective-permute-start(f32[32,66,1]{1,0,2:T(8,128)} %copy.248), channel_id=1, source_target_pairs={{0,1},{1,2},{2,3},{4,5},{5,6},{6,7},{8,9},{9,10},{10,11},{12,13},{... | collective-permute-start | bytes 25352 | tf_op jit(solution)/shard_map/ppermute | solution.py:25
  168.2 13.2 %collective-permute-start.19 = (f32[32,66,1]{1,0,2:T(8,128)}, f32[32,66,1]{1,0,2:T(8,128)}, u32[]{:S(2)}, u32[]{:S(2)}) collective-permute-start(f32[32,66,1]{1,0,2:T(8,128)} %copy.249), channel_id=1, source_target_pairs={{1,0},{2,1},{3,2},{5,4},{6,5},{7,6},{9,8},{10,9},{11,10},{13,12},{... | collective-permute-start | bytes 25352 | tf_op jit(solution)/shard_map/ppermute | solution.py:26
  183.7 3.6 copy-start.21
  183.7 3.6 copy-start.32
  183.7 3.6 copy-start.37
  183.7 3.6 copy-start.50
  183.7 3.6 copy-start.52
  215.3 8.0 %copy-start.55 = (f32[2,32]{1,0:T(2,128)S(1)}, f32[2,32]{1,0:T(2,128)}, u32[]{:S(2)}) copy-start(f32[2,32]{1,0:T(2,128)} %param.23) | copy-start | bytes 772
  215.3 77.1 %copy-start.54 = (s32[1024]{0:T(1024)S(1)}, s32[1024]{0:T(1024)}, u32[]{:S(2)}) copy-start(s32[1024]{0:T(1024)} %param.18) | copy-start | bytes 12292
  215.3 92.0 %all-to-all-start = ((bf16[32,16,2048]{2,1,0:T(8,128)(2,1)}), bf16[32,16,2048]{2,1,0:T(8,128)(2,1)S(1)}, u32[]{:S(2)}, u32[]{:S(2)}) async-start(bf16[32,16,2048]{2,1,0:T(8,128)(2,1)} %bitcast.32), calls=%async_computation | async-start | bytes 4194304 | tf_op jit(solution)/shard_map/all_to_all | solution.py:123
  223.3 295.0 %all-reduce.8.cloned.1.call-start = ((), (), s32[]{:S(2)}) async-start(), calls=%async_computation.3 | async-start | bytes 16777216 | tf_op jit(solution)/shard_map/psum | solution.py:143
  307.4 5.9 %copy-start.26 = (bf16[1024,2048]{1,0:T(8,128)(2,1)S(1)}, bf16[1024,2048]{1,0:T(8,128)(2,1)}, u32[]{:S(2)}) copy-start(bf16[1024,2048]{1,0:T(8,128)(2,1)} %gather_fusion) | copy-start | bytes 12582916
  307.4 5.9 %copy-start.59 = (bf16[2,1024,1024]{2,1,0:T(8,128)(2,1)S(1)}, bf16[2,1024,1024]{2,1,0:T(8,128)(2,1)}, u32[]{:S(2)}) copy-start(bf16[2,1024,1024]{2,1,0:T(8,128)(2,1)} %all-gather.3.cloned.1.call-done) | copy-start | bytes 12582916
  335.7 45.5 %copy-start.56 = (f32[2,32]{1,0:T(2,128)S(1)}, f32[2,32]{1,0:T(2,128)}, u32[]{:S(2)}) copy-start(f32[2,32]{1,0:T(2,128)} %param.24) | copy-start | bytes 772
  335.7 45.5 %copy-start.57 = (f32[2,32]{1,0:T(2,128)S(1)}, f32[2,32]{1,0:T(2,128)}, u32[]{:S(2)}) copy-start(f32[2,32]{1,0:T(2,128)} %param.25) | copy-start | bytes 772
  335.7 182.6 %copy-start.27 = (f32[2,32,1024]{2,1,0:T(8,128)S(1)}, f32[2,32,1024]{2,1,0:T(8,128)}, u32[]{:S(2)}) copy-start(f32[2,32,1024]{2,1,0:T(8,128)} %param.20) | copy-start | bytes 786436
  335.7 182.6 %copy-start.39 = (f32[2,32,1024]{2,1,0:T(8,128)S(1)}, f32[2,32,1024]{2,1,0:T(8,128)}, u32[]{:S(2)}) copy-start(f32[2,32,1024]{2,1,0:T(8,128)} %param.21) | copy-start | bytes 786436
  335.7 182.6 %copy-start.40 = (f32[2,32,1024]{2,1,0:T(8,128)S(1)}, f32[2,32,1024]{2,1,0:T(8,128)}, u32[]{:S(2)}) copy-start(f32[2,32,1024]{2,1,0:T(8,128)} %param.22) | copy-start | bytes 786436
  (20 other events, 46.9 us)
Sparse Core Ops, SparseCore 0:
  23.0 65.4 all-gather.2
  335.8 182.3 all-reduce.7
where the time goes:
time: 536 us; the launch traced here: 527 us
  waiting for transfers between devices  144 us (27%)
  blocking collectives  114 us (21%)
  local copies, waits for them, and re-layouts  98.1 us (18%)
  starting transfers between devices  70.7 us (13%)
  other arithmetic  60.8 us (11%)
  matrix products  24.1 us (4%)
  between operations  15.2 us (3%)
    psum x1, waiting for transfers between devices, local(): whole_w, whole_b = lax.psum((grad_w, grad_b), ('gx', 'gy'))  136 us
    all_gather x1, blocking collectives, local(): lax.all_gather(biases.astype(jnp.bfloat16), ('gx', 'gy'), axis=1, tiled=T...  69 us
    psum x1, blocking collectives, local(): whole_w, whole_b = lax.psum((grad_w, grad_b), ('gx', 'gy'))  45.4 us
    ppermute x10, starting transfers between devices, with_halo(): before = lax.ppermute(last, axis, up)  39.4 us
    add x4, other arithmetic, update(): return centre + time_step * (flux - rate_inner * centre)  21.1 us
    concatenate x10, other arithmetic, with_halo(): x = jnp.concatenate([before, x, after], axis=dim)  18.8 us
    slice x9, local copies, waits for them, and re-layouts, with_halo(): first = lax.slice_in_dim(x, 0, width, axis=dim)  14.2 us
    gather x1, local copies, waits for them, and re-layouts, local(): rows = jnp.concatenate([reservoir[res_slot], arrived], 0)  13.5 us
  transfers between devices with their start and end apart: 24, of which 3 were waited for; matrix products, arithmetic and copies ran while one was open for 28% of the time, Pallas kernels for 0%

commit v1 on v0

--- a/solution.py
+++ b/solution.py
@@ -50,8 +50,8 @@
     return jnp.pad(array, ((1, 1), (0, 0), (0, 0)))
 
 
-def local_grads(rows, live, wbf, bbf):
-    width = wbf.shape[1]
+def local_grads(rows, count, wbf, bbf):
+    width = wbf[0].shape[1]
     inputs = rows[:, :width]
     target = rows[:, width:].astype(jnp.float32)
     pre = jnp.dot(inputs, wbf[0], preferred_element_type=jnp.float32) + bbf[0].astype(jnp.float32)
@@ -60,15 +60,14 @@
     pred = jnp.dot(hidden_b, wbf[1], preferred_element_type=jnp.float32) + bbf[1].astype(
         jnp.float32
     )
-    count = jnp.sum(live)
-    grad_pred = 2.0 * (pred - target) * live[:, None] / count
+    grad_pred = 2.0 * (pred - target) / count[:, None]
     grad_pred_b = grad_pred.astype(jnp.bfloat16)
     grad_w2 = jnp.dot(hidden_b.T, grad_pred_b, preferred_element_type=jnp.float32)
     grad_hid = jnp.dot(grad_pred_b, wbf[1].T, preferred_element_type=jnp.float32)
     grad_pre = grad_hid * (1.0 - hidden * hidden)
     grad_pre_b = grad_pre.astype(jnp.bfloat16)
     grad_w1 = jnp.dot(inputs.T, grad_pre_b, preferred_element_type=jnp.float32)
-    return (jnp.stack([grad_w1, grad_w2]), jnp.stack([jnp.sum(grad_pre, 0), jnp.sum(grad_pred, 0)]))
+    return grad_w1, grad_w2, jnp.stack([jnp.sum(grad_pre, 0), jnp.sum(grad_pred, 0)])
 
 
 def adam(param, moment, second, grad):
@@ -102,48 +101,29 @@
         state = update(zpad(padded), kpad, rate)
     devices = lax.axis_size("gx") * lax.axis_size("gy")
     count_dev = patch_cell.shape[0]
-    cap = max(2, 2 * count_dev // devices)
     stacked = jnp.stack([field, state]).reshape(2, depth, cells_x * cells_y // PW, PW)
     picked = stacked[:, :, patch_cell, :]
     patches = (
         jnp.transpose(picked, (2, 0, 1, 3)).reshape(count_dev, 2 * depth * PW).astype(jnp.bfloat16)
     )
-    target_of = trainer[:, 0]
-    onehot = (target_of[:, None] == jnp.arange(devices, dtype=jnp.int32)[None, :]).astype(jnp.int32)
-    rank = jnp.sum(jnp.cumsum(onehot, 0) * onehot, 1) - 1
-    where_to = target_of * cap + rank
-    width2 = patches.shape[1]
-    outbox = jnp.zeros((devices * cap, width2), jnp.bfloat16).at[where_to].set(patches)
-    flags = (
-        jnp.zeros((devices * cap,), jnp.bfloat16)
-        .at[where_to]
-        .set(jnp.ones((count_dev,), jnp.bfloat16))
+    axes = ("gx", "gy")
+    onehot = (trainer == jnp.arange(devices, dtype=jnp.int32)[None, :]).astype(jnp.float32)
+    stored = res_slot.shape[0]
+    total = stored + lax.psum(jnp.sum(onehot, 0), axes)
+    mine = lax.axis_index("gx") * lax.axis_size("gy") + lax.axis_index("gy")
+    own = total[mine]
+    count = jnp.concatenate(
+        [jnp.full((stored,), stored, jnp.float32) - stored + own, jnp.sum(onehot * total, 1)]
     )
-    arrived, alive = (
-        lax.all_to_all(
-            outbox.reshape(devices, cap, width2),
-            ("gx", "gy"),
-            split_axis=0,
-            concat_axis=0,
-            tiled=True,
-        ),
-        lax.all_to_all(
-            flags.reshape(devices, cap), ("gx", "gy"), split_axis=0, concat_axis=0, tiled=True
-        ),
+    wbf = [lax.all_gather(weights[i].astype(jnp.bfloat16), axes, axis=0, tiled=True) for i in (0, 1)]
+    bbf = lax.all_gather(biases.astype(jnp.bfloat16), axes, axis=1, tiled=True)
+    rows = jnp.concatenate([reservoir[res_slot], patches], 0)
+    grad_1, grad_2, grad_b = local_grads(rows, count, wbf, bbf)
+    share_w = jnp.stack(
+        [lax.psum_scatter(g, axes, scatter_dimension=0, tiled=True) for g in (grad_1, grad_2)]
     )
-    arrived = arrived.reshape(devices * cap, width2)
-    alive = alive.reshape(devices * cap).astype(jnp.float32)
-    wfull, bfull = (
-        lax.all_gather(weights.astype(jnp.bfloat16), ("gx", "gy"), axis=1, tiled=True),
-        lax.all_gather(biases.astype(jnp.bfloat16), ("gx", "gy"), axis=1, tiled=True),
-    )
-    rows = jnp.concatenate([reservoir[res_slot], arrived], 0)
-    live = jnp.concatenate([jnp.ones((res_slot.shape[0],), jnp.float32), alive])
-    grad_w, grad_b = local_grads(rows, live, wfull, bfull)
-    whole_w, whole_b = lax.psum((grad_w, grad_b), ("gx", "gy"))
-    position = lax.axis_index("gx") * lax.axis_size("gy") + lax.axis_index("gy")
-    share_w = lax.dynamic_slice_in_dim(whole_w, position * weights.shape[1], weights.shape[1], 1)
-    share_b = lax.dynamic_slice_in_dim(whole_b, position * biases.shape[1], biases.shape[1], 1)
+    whole_b = lax.psum(grad_b, axes)
+    share_b = lax.dynamic_slice_in_dim(whole_b, mine * biases.shape[1], biases.shape[1], 1)
     new_w, new_wm, new_wv = adam(weights, w_mom, w_var, share_w)
     new_b, new_bm, new_bv = adam(biases, b_mom, b_var, share_b)
     return (state, new_w, new_wm, new_wv, new_b, new_bm, new_bv)

time: 536 us -> 609 us (1.14)
  waiting for transfers between devices: 144 us -> 229 us
  starting transfers between devices: 70.7 us -> 53.3 us
  blocking collectives: 114 us -> 126 us
  local copies, waits for them, and re-layouts: 98.1 us -> 90.1 us
  matrix products: 24.1 us -> 31.1 us
  other arithmetic: 60.8 us -> 54.6 us
    reduce_scatter x0 -> x2, waiting for transfers between devices: none -> 227 us  [local(): lax.psum_scatter(g, axes, scatter_dimension=0, tiled=True)]
    psum x1 -> x0, waiting for transfers between devices: 136 us -> none  [local(): whole_w, whole_b = lax.psum((grad_w, grad_b), ('gx', 'gy'))]
    psum x1 -> x2, blocking collectives: 45.4 us -> 86.8 us  [the longest x1 46 us: local(): whole_b = lax.psum(grad_b, axes)]
    all_gather x1, blocking collectives: 69 us -> 39.2 us  [local(): bbf = lax.all_gather(biases.astype(jnp.bfloat16), axes, axis=1, tiled=True)]
    all_to_all x2 -> x0, starting transfers between devices: 17.9 us -> none  [the longest x1 9.96 us: local(): lax.all_to_all(flags.reshape(devices, cap), ('gx', 'gy'), split_axis=0, c...]
    scatter x2 -> x0, local copies, waits for them, and re-layouts: 6.69 us -> none  [the longest x1 3.85 us: local(): jnp.zeros((devices * cap, width2), jnp.bfloat16).at[where_to].set(patches)]
    ppermute x10, waiting for transfers between devices: 7.52 us -> 0.87 us  [with_halo(): after = lax.ppermute(first, axis, down)]
  transfers between devices with their start and end apart: 24 -> 24, of which waited for: 3 -> 5; matrix products, arithmetic and copies ran while one was open for 28% -> 26% of each run, Pallas kernels for 0% -> 0%
where the time goes in v1:
time: 609 us; the launch traced here: 600 us
  waiting for transfers between devices  229 us (38%)
  blocking collectives  126 us (21%)
  local copies, waits for them, and re-layouts  90.1 us (15%)
  other arithmetic  54.6 us (9%)
  starting transfers between devices  53.3 us (9%)
  matrix products  31.1 us (5%)
  between operations  15.1 us (2%)
    reduce_scatter x2, waiting for transfers between devices, local(): lax.psum_scatter(g, axes, scatter_dimension=0, tiled=True)  227 us
    psum x1, blocking collectives, local(): whole_b = lax.psum(grad_b, axes)  46 us
    psum x1, blocking collectives, local(): total = stored + lax.psum(jnp.sum(onehot, 0), axes)  40.8 us
    ppermute x10, starting transfers between devices, with_halo(): before = lax.ppermute(last, axis, up)  39.8 us
    all_gather x1, blocking collectives, local(): bbf = lax.all_gather(biases.astype(jnp.bfloat16), axes, axis=1, tiled=True)  39.2 us
    add x4, other arithmetic, update(): return centre + time_step * (flux - rate_inner * centre)  21.8 us
    concatenate x10, other arithmetic, with_halo(): x = jnp.concatenate([before, x, after], axis=dim)  19.4 us
    slice x9, local copies, waits for them, and re-layouts, with_halo(): first = lax.slice_in_dim(x, 0, width, axis=dim)  14.8 us
  transfers between devices with their start and end apart: 24, of which 5 were waited for; matrix products, arithmetic and copies ran while one was open for 26% of the time, Pallas kernels for 0%

profile of v1, /device:TPU:0, one launch (start us, length us, event | category | flops | bytes accessed | tf_op | source)
XLA Modules:
  0.0 599.6 jit_solution(6986619607021737462)
XLA Ops:
  11.2 5.5 collective-permute-start.4
  19.0 5.4 collective-permute-start
  25.2 39.2 %all-gather.2 = bf16[32,32,2]{1,2,0:T(2,128)(2,1)S(1)} all-gather(bf16[1,32,2]{1,2,0:T(2,128)(2,1)S(1)} %convert_bitcast_fusion), channel_id=1, replica_groups=mesh['gx'=8,'gy'=4] {'gx','gy'}, dimensions={0}, use_global_device_ids=true | all-gather | bytes 4224 | tf_op jit(solution)/shard_map/all_gather | solution.py:119
  65.1 1.3 pad_maximum_fusion.3
  67.3 2.2 collective-permute-start.6
  71.4 1.4 fusion.106
  72.8 1.8 copy.189
  76.3 3.7 collective-permute-start.2
  80.6 1.6 copy.199
  82.1 3.8 select_maximum_fusion.12
  86.0 1.5 copy.191
  87.5 1.5 copy.190
  89.1 2.9 select_maximum_fusion.16
  92.4 5.8 fusion.71
  99.5 4.5 collective-permute-start.8
  105.6 1.8 fusion.105
  107.4 2.3 copy.212
  109.7 3.1 collective-permute-start.10
  112.8 2.3 copy.213
  115.1 1.5 collective-permute-start.11
  116.5 1.3 convert_reduce_fusion
  117.9 2.2 copy.214
  120.1 2.2 copy.215
  122.4 3.2 select_maximum_fusion.8
  126.0 5.1 fusion.53
  134.0 5.2 collective-permute-start.12
  139.7 40.8 %psum.14 = f32[32]{0:T(128)} all-reduce(f32[32]{0:T(128)} %convert_reduce_fusion), channel_id=1, replica_groups=mesh['gx'=8,'gy'=4] {'gx','gy'}, use_global_device_ids=true, to_apply=%region_1.2 | all-reduce | flops 32 | bytes 256 | tf_op jit(solution)/shard_map/psum | solution.py:112
  180.6 1.4 pad_maximum_fusion.5
  181.9 1.8 fusion.104
  183.7 2.3 copy.224
  186.0 1.9 collective-permute-start.14
  187.9 2.3 copy.225
  192.7 2.2 copy.226
  195.7 2.2 copy.227
  198.0 3.2 select_maximum_fusion.4
  201.6 5.1 fusion.35
  208.1 4.5 collective-permute-start.16
  214.8 1.8 fusion.103
  216.6 2.3 copy.236
  218.9 3.8 collective-permute-start.18
  222.7 2.3 copy.237
  225.0 1.5 collective-permute-start.19
  227.8 3.7 stack.27
  232.8 4.3 copy.244
  238.3 13.4 %gather_fusion = bf16[1024,2048]{1,0:T(8,128)(2,1)} fusion(bf16[2048,2048]{1,0:T(8,128)(2,1)} %param.19, s32[1024]{0:T(1024)} %fusion.97), kind=kCustom, calls=%fused_computation | custom fusion | bytes 8392704 | tf_op jit(solution)/shard_map/gather | solution.py:120
  251.7 2.2 copy.238
  254.0 2.3 copy.239
  256.3 3.2 select_maximum_fusion
  259.9 5.8 fusion.17
  265.7 2.7 stack.28
  268.4 1.4 copy.245
  270.0 3.0 pad_maximum_fusion
  273.0 5.5 gather_fusion.1
  278.5 5.1 copy.246
  284.3 7.4 %fusion.7 = f32[1280,1024]{1,0:T(8,128)} fusion(bf16[1,1024,1024]{2,1,0:T(8,128)(2,1)} %all-gather.6.cloned.1.call-done, bf16[1024,2048]{1,0:T(8,128)(2,1)} %gather_fusion, bf16[256,2048]{1,0:T(8,128)(2,1)S(1)} %copy.247), kind=kOutput, calls=%fused_computation.38 | convolution fusion | flops 2689597440 | bytes 12582912 | tf_op jit(solution)/shard_map/dot_general | solution.py:57
  291.8 7.3 %fusion.114 = (f32[1024]{0:T(1024)S(1)}, bf16[1280,1024]{1,0:T(8,128)(2,1)S(1)}) fusion(f32[1280]{0:T(1024)S(1)} %copy-done.53, bf16[256,2048]{1,0:T(8,128)(2,1)S(1)} %copy.247, bf16[1024,2048]{1,0:T(8,128)(2,1)} %gather_fusion, f32[1024]{0:T(1024)S(1)} %bitcast.106, bf16[1,1024,1024]{2,1,0:T(8,128)(2,1)} %all-gather.8.cloned.1.call-done, ...), kind=kOutput, calls=%fused_computation.212 | convolution fusion | flops 2700082176 | bytes 15221760 | tf_op jit(solution)/shard_map/dot_general | solution.py:60
  299.1 1.4 copy-done.65
  300.6 4.5 fusion.9
  305.2 7.4 %fusion.115 = (f32[1024]{0:T(1024)S(1)}, bf16[1280,1024]{1,0:T(8,128)(2,1)S(1)}) fusion(f32[1280,1024]{1,0:T(8,128)} %fusion.7, f32[1024]{0:T(1024)S(1)} %bitcast.105, bf16[1,1024,1024]{2,1,0:T(8,128)(2,1)} %all-gather.8.cloned.1.call-done, bf16[1280,1024]{1,0:T(8,128)(2,1)} %copy-done.65), kind=kOutput, calls=%fused_computation.213 | convolution fusion | flops 2692217856 | bytes 12591104 | tf_op jit(solution)/shard_map/dot_general | solution.py:66
  312.6 4.5 fusion.2
  317.2 46.0 %psum.15 = f32[2,1024]{1,0:T(2,128)S(1)} all-reduce(f32[2,1024]{1,0:T(2,128)S(1)} %pad_maximum_fusion.48), channel_id=1, replica_groups=mesh['gx'=8,'gy'=4] {'gx','gy'}, use_global_device_ids=true, to_apply=%region_7.8 | all-reduce | flops 2048 | bytes 16384 | tf_op jit(solution)/shard_map/psum | solution.py:125
  363.8 87.5 %reduce-scatter.5.cloned.1.call-done = f32[32,1024]{1,0:T(8,128)} async-done(((f32[1024,1024]{1,0:T(8,128)}), f32[32,1024]{1,0:T(8,128)}) %reduce-scatter.5.cloned.1.call-update) | async-done | bytes 131088 | tf_op jit(solution)/shard_map/reduce_scatter | solution.py:123
  451.4 139.4 %reduce-scatter.3.cloned.1.call-done = f32[32,1024]{1,0:T(8,128)} async-done(((f32[1024,1024]{1,0:T(8,128)}), f32[32,1024]{1,0:T(8,128)}) %reduce-scatter.3.cloned.1.call-update) | async-done | bytes 131088 | tf_op jit(solution)/shard_map/reduce_scatter | solution.py:123
  590.7 1.9 divide_subtract_fusion
  (198 shorter events, 32.8 us)
Async XLA Ops:
  7.2 277.2 %all-gather.6.cloned.1.call-start = ((), (), s32[]{:S(2)}) async-start(), calls=%async_computation.4 | async-start | bytes 2162688 | tf_op jit(solution)/shard_map/all_gather | solution.py:118
  8.9 282.9 %all-gather.8.cloned.1.call-start = ((), (), s32[]{:S(2)}) async-start(), calls=%async_computation.5 | async-start | bytes 2162688 | tf_op jit(solution)/shard_map/all_gather | solution.py:118
  9.9 55.2 %collective-permute-start.5 = (f32[32,1,128]{2,0,1:T(8,128)S(1)}, f32[32,1,128]{2,0,1:T(8,128)S(1)}, u32[]{:S(2)}, u32[]{:S(2)}) collective-permute-start(f32[32,1,128]{2,0,1:T(8,128)S(1)} %bitcast.98), channel_id=1, source_target_pairs={{4,0},{8,4},{12,8},{16,12},{20,16},{24,20},{28,24},{5,1},{9,5},{13... | collective-permute-start | bytes 49160 | tf_op jit(solution)/shard_map/ppermute | solution.py:26
  11.2 53.9 %collective-permute-start.4 = (f32[32,1,128]{2,0,1:T(8,128)S(1)}, f32[32,1,128]{2,0,1:T(8,128)S(1)}, u32[]{:S(2)}, u32[]{:S(2)}) collective-permute-start(f32[32,1,128]{2,0,1:T(8,128)S(1)} %bitcast.97), channel_id=1, source_target_pairs={{0,4},{4,8},{8,12},{12,16},{16,20},{20,24},{24,28},{1,5},{5,9},{9,... | collective-permute-start | bytes 49160 | tf_op jit(solution)/shard_map/ppermute | solution.py:25
  17.7 53.5 %collective-permute-start.1 = (f32[32,1,128]{2,0,1:T(8,128)S(1)}, f32[32,1,128]{2,0,1:T(8,128)S(1)}, u32[]{:S(2)}, u32[]{:S(2)}) collective-permute-start(f32[32,1,128]{2,0,1:T(8,128)S(1)} %bitcast.96), channel_id=1, source_target_pairs={{4,0},{8,4},{12,8},{16,12},{20,16},{24,20},{28,24},{5,1},{9,5},{13... | collective-permute-start | bytes 49160 | tf_op jit(solution)/shard_map/ppermute | solution.py:26
  19.0 52.3 %collective-permute-start = (f32[32,1,128]{2,0,1:T(8,128)S(1)}, f32[32,1,128]{2,0,1:T(8,128)S(1)}, u32[]{:S(2)}, u32[]{:S(2)}) collective-permute-start(f32[32,1,128]{2,0,1:T(8,128)S(1)} %bitcast.95), channel_id=1, source_target_pairs={{0,4},{4,8},{8,12},{12,16},{16,20},{20,24},{24,28},{1,5},{5,9},{9,... | collective-permute-start | bytes 49160 | tf_op jit(solution)/shard_map/ppermute | solution.py:25
  24.5 426.9 %reduce-scatter.5.cloned.1.call-start = ((), (), s32[]{:S(2)}) async-start(), calls=%async_computation.3 | async-start | bytes 4325376 | tf_op jit(solution)/shard_map/reduce_scatter | solution.py:123
  65.1 17.0 %copy-start.41 = (f32[32,1,128]{2,0,1:T(8,128)}, f32[32,1,128]{2,0,1:T(8,128)S(1)}, u32[]{:S(2)}) copy-start(f32[32,1,128]{2,0,1:T(8,128)S(1)} %collective-permute-done.5) | copy-start | bytes 49156
  65.1 17.0 %copy-start.43 = (f32[32,1,128]{2,0,1:T(8,128)}, f32[32,1,128]{2,0,1:T(8,128)S(1)}, u32[]{:S(2)}) copy-start(f32[32,1,128]{2,0,1:T(8,128)S(1)} %collective-permute-done.4) | copy-start | bytes 49156
  66.5 4.8 copy-start.8
  67.3 12.7 %collective-permute-start.6 = (f32[32,66,1]{1,0,2:T(8,128)S(1)}, f32[32,66,1]{1,0,2:T(8,128)S(1)}, u32[]{:S(2)}, u32[]{:S(2)}) collective-permute-start(f32[32,66,1]{1,0,2:T(8,128)S(1)} %copy.196), channel_id=1, source_target_pairs={{0,1},{1,2},{2,3},{4,5},{5,6},{6,7},{8,9},{9,10},{10,11},{12,13},{... | collective-permute-start | bytes 25352 | tf_op jit(solution)/shard_map/ppermute | solution.py:25
  69.9 10.6 %collective-permute-start.7 = (f32[32,66,1]{1,0,2:T(8,128)S(1)}, f32[32,66,1]{1,0,2:T(8,128)S(1)}, u32[]{:S(2)}, u32[]{:S(2)}) collective-permute-start(f32[32,66,1]{1,0,2:T(8,128)S(1)} %copy.197), channel_id=1, source_target_pairs={{1,0},{2,1},{3,2},{5,4},{6,5},{7,6},{9,8},{10,9},{11,10},{13,12},{... | collective-permute-start | bytes 25352 | tf_op jit(solution)/shard_map/ppermute | solution.py:26
  72.8 9.3 %copy-start.9 = (f32[32,64,128]{2,1,0:T(8,128)S(1)}, f32[32,64,128]{2,1,0:T(8,128)}, u32[]{:S(2)}) copy-start(f32[32,64,128]{2,1,0:T(8,128)} %param.13) | copy-start | bytes 3145732
  74.6 11.4 %collective-permute-start.3 = (f32[32,66,1]{1,0,2:T(8,128)S(1)}, f32[32,66,1]{1,0,2:T(8,128)S(1)}, u32[]{:S(2)}, u32[]{:S(2)}) collective-permute-start(f32[32,66,1]{1,0,2:T(8,128)S(1)} %copy.189), channel_id=1, source_target_pairs={{1,0},{2,1},{3,2},{5,4},{6,5},{7,6},{9,8},{10,9},{11,10},{13,12},{... | collective-permute-start | bytes 25352 | tf_op jit(solution)/shard_map/ppermute | solution.py:26
  76.3 11.1 %collective-permute-start.2 = (f32[32,66,1]{1,0,2:T(8,128)S(1)}, f32[32,66,1]{1,0,2:T(8,128)S(1)}, u32[]{:S(2)}, u32[]{:S(2)}) collective-permute-start(f32[32,66,1]{1,0,2:T(8,128)S(1)} %copy.188), channel_id=1, source_target_pairs={{0,1},{1,2},{2,3},{4,5},{5,6},{6,7},{8,9},{9,10},{10,11},{12,13},{... | collective-permute-start | bytes 25352 | tf_op jit(solution)/shard_map/ppermute | solution.py:25
  80.6 5.4 copy-start.21
  89.0 3.3 copy-start.22
  89.0 3.3 copy-start.30
  89.0 3.3 copy-start.35
  92.4 11.7 %copy-start.55 = (s32[1024]{0:T(1024)S(1)}, s32[1024]{0:T(1024)}, u32[]{:S(2)}) copy-start(s32[1024]{0:T(1024)} %param.18) | copy-start | bytes 12292
  98.1 9.2 %copy-start.15 = (f32[32,64,128]{2,1,0:T(8,128)}, f32[32,64,128]{2,1,0:T(8,128)S(1)}, u32[]{:S(2)}) copy-start(f32[32,64,128]{2,1,0:T(8,128)S(1)} %fusion.71) | copy-start | bytes 3145732
  98.2 6.5 %collective-permute-start.9 = (f32[32,1,128]{2,0,1:T(8,128)S(1)}, f32[32,1,128]{2,0,1:T(8,128)S(1)}, u32[]{:S(2)}, u32[]{:S(2)}) collective-permute-start(f32[32,1,128]{2,0,1:T(8,128)S(1)} %bitcast.101), channel_id=1, source_target_pairs={{4,0},{8,4},{12,8},{16,12},{20,16},{24,20},{28,24},{5,1},{9,5},{13... | collective-permute-start | bytes 49160 | tf_op jit(solution)/shard_map/ppermute | solution.py:26
  99.5 6.0 collective-permute-start.8
  109.7 8.2 %collective-permute-start.10 = (f32[32,66,1]{1,0,2:T(8,128)}, f32[32,66,1]{1,0,2:T(8,128)}, u32[]{:S(2)}, u32[]{:S(2)}) collective-permute-start(f32[32,66,1]{1,0,2:T(8,128)} %copy.212), channel_id=1, source_target_pairs={{0,1},{1,2},{2,3},{4,5},{5,6},{6,7},{8,9},{9,10},{10,11},{12,13},{... | collective-permute-start | bytes 25352 | tf_op jit(solution)/shard_map/ppermute | solution.py:25
  115.1 5.0 collective-permute-start.11
  122.3 3.3 copy-start.18
  122.3 3.7 copy-start.24
  122.3 3.7 copy-start.31
  122.4 3.7 copy-start.36
  122.4 3.7 copy-start.50
  122.4 3.7 copy-start.52
  126.0 13.1 %copy-start.61 = (s32[256]{0:T(256)S(1)}, s32[256]{0:T(256)}, u32[]{:S(2)}) copy-start(s32[256]{0:T(256)} %param.16) | copy-start | bytes 3076
  132.7 47.9 %collective-permute-start.13 = (f32[32,1,128]{2,0,1:T(8,128)}, f32[32,1,128]{2,0,1:T(8,128)}, u32[]{:S(2)}, u32[]{:S(2)}) collective-permute-start(f32[32,1,128]{2,0,1:T(8,128)} %bitcast.16), channel_id=1, source_target_pairs={{4,0},{8,4},{12,8},{16,12},{20,16},{24,20},{28,24},{5,1},{9,5},{13... | collective-permute-start | bytes 49160 | tf_op jit(solution)/shard_map/ppermute | solution.py:26
  134.0 46.6 %collective-permute-start.12 = (f32[32,1,128]{2,0,1:T(8,128)}, f32[32,1,128]{2,0,1:T(8,128)}, u32[]{:S(2)}, u32[]{:S(2)}) collective-permute-start(f32[32,1,128]{2,0,1:T(8,128)} %bitcast.14), channel_id=1, source_target_pairs={{0,4},{4,8},{8,12},{12,16},{16,20},{20,24},{24,28},{1,5},{5,9},{9,... | collective-permute-start | bytes 49160 | tf_op jit(solution)/shard_map/ppermute | solution.py:25
  186.0 6.6 %collective-permute-start.14 = (f32[32,66,1]{1,0,2:T(8,128)}, f32[32,66,1]{1,0,2:T(8,128)}, u32[]{:S(2)}, u32[]{:S(2)}) collective-permute-start(f32[32,66,1]{1,0,2:T(8,128)} %copy.224), channel_id=1, source_target_pairs={{0,1},{1,2},{2,3},{4,5},{5,6},{6,7},{8,9},{9,10},{10,11},{12,13},{... | collective-permute-start | bytes 25352 | tf_op jit(solution)/shard_map/ppermute | solution.py:25
  190.2 5.5 collective-permute-start.15
  198.0 3.6 copy-start.25
  198.0 3.6 copy-start.32
  198.0 3.6 copy-start.37
  201.6 11.1 %copy-start.62 = (s32[256,1]{0,1:T(1,128)S(1)}, s32[256,1]{0,1:T(1,128)}, u32[]{:S(2)}) copy-start(s32[256,1]{0,1:T(1,128)} %param.17) | copy-start | bytes 3076
  201.6 11.1 %copy-start.63 = (f32[32]{0:T(128)S(1)}, f32[32]{0:T(128)}, u32[]{:S(2)}) copy-start(f32[32]{0:T(128)} %broadcast_add_fusion) | copy-start | bytes 388
  206.8 9.8 %copy-start.11 = (f32[32,64,128]{2,1,0:T(8,128)}, f32[32,64,128]{2,1,0:T(8,128)S(1)}, u32[]{:S(2)}) copy-start(f32[32,64,128]{2,1,0:T(8,128)S(1)} %fusion.35) | copy-start | bytes 3145732
  206.8 6.5 %collective-permute-start.17 = (f32[32,1,128]{2,0,1:T(8,128)S(1)}, f32[32,1,128]{2,0,1:T(8,128)S(1)}, u32[]{:S(2)}, u32[]{:S(2)}) collective-permute-start(f32[32,1,128]{2,0,1:T(8,128)S(1)} %bitcast.102), channel_id=1, source_target_pairs={{4,0},{8,4},{12,8},{16,12},{20,16},{24,20},{28,24},{5,1},{9,5},{13... | collective-permute-start | bytes 49160 | tf_op jit(solution)/shard_map/ppermute | solution.py:26
  208.1 6.0 collective-permute-start.16
  218.9 32.8 %collective-permute-start.18 = (f32[32,66,1]{1,0,2:T(8,128)}, f32[32,66,1]{1,0,2:T(8,128)}, u32[]{:S(2)}, u32[]{:S(2)}) collective-permute-start(f32[32,66,1]{1,0,2:T(8,128)} %copy.236), channel_id=1, source_target_pairs={{0,1},{1,2},{2,3},{4,5},{5,6},{6,7},{8,9},{9,10},{10,11},{12,13},{... | collective-permute-start | bytes 25352 | tf_op jit(solution)/shard_map/ppermute | solution.py:25
  225.0 28.9 %collective-permute-start.19 = (f32[32,66,1]{1,0,2:T(8,128)}, f32[32,66,1]{1,0,2:T(8,128)}, u32[]{:S(2)}, u32[]{:S(2)}) collective-permute-start(f32[32,66,1]{1,0,2:T(8,128)} %copy.237), channel_id=1, source_target_pairs={{1,0},{2,1},{3,2},{5,4},{6,5},{7,6},{9,8},{10,9},{11,10},{13,12},{... | collective-permute-start | bytes 25352 | tf_op jit(solution)/shard_map/ppermute | solution.py:26
  231.5 5.5 copy-start.54
  256.2 3.6 copy-start.23
  256.2 3.6 copy-start.33
  256.3 3.6 copy-start.38
  256.3 3.6 copy-start.46
  256.3 3.6 copy-start.48
  284.3 7.5 %copy-start.53 = (f32[1280]{0:T(1024)S(1)}, f32[1280]{0:T(1024)}, u32[]{:S(2)}) copy-start(f32[1280]{0:T(1024)} %concatenate.128) | copy-start | bytes 15364
  284.3 7.5 %copy-start.56 = (f32[1,1024]{1,0:T(1,128)S(1)}, f32[1,1024]{1,0:T(1,128)}, u32[]{:S(2)}) copy-start(f32[1,1024]{1,0:T(1,128)} %get-tuple-element.56) | copy-start | bytes 12292
  284.3 7.5 %copy-start.57 = (f32[1,1024]{1,0:T(1,128)S(1)}, f32[1,1024]{1,0:T(1,128)}, u32[]{:S(2)}) copy-start(f32[1,1024]{1,0:T(1,128)} %get-tuple-element.57) | copy-start | bytes 12292
  291.8 8.8 %copy-start.64 = (f32[1280,1024]{1,0:T(8,128)S(1)}, f32[1280,1024]{1,0:T(8,128)}, u32[]{:S(2)}) copy-start(f32[1280,1024]{1,0:T(8,128)} %fusion.7) | copy-start | bytes 15728644
  305.1 285.6 %reduce-scatter.3.cloned.1.call-start = ((), (), s32[]{:S(2)}) async-start(), calls=%async_computation.2 | async-start | bytes 4325376 | tf_op jit(solution)/shard_map/reduce_scatter | solution.py:123
  305.1 7.4 %copy-start.27 = (bf16[1024,2048]{1,0:T(8,128)(2,1)S(1)}, bf16[1024,2048]{1,0:T(8,128)(2,1)}, u32[]{:S(2)}) copy-start(bf16[1024,2048]{1,0:T(8,128)(2,1)} %gather_fusion) | copy-start | bytes 12582916
  317.1 46.1 %copy-start.58 = (f32[2,32]{1,0:T(2,128)S(1)}, f32[2,32]{1,0:T(2,128)}, u32[]{:S(2)}) copy-start(f32[2,32]{1,0:T(2,128)} %param.23) | copy-start | bytes 772
  317.1 46.1 %copy-start.59 = (f32[2,32]{1,0:T(2,128)S(1)}, f32[2,32]{1,0:T(2,128)}, u32[]{:S(2)}) copy-start(f32[2,32]{1,0:T(2,128)} %param.24) | copy-start | bytes 772
  317.1 46.1 %copy-start.60 = (f32[2,32]{1,0:T(2,128)S(1)}, f32[2,32]{1,0:T(2,128)}, u32[]{:S(2)}) copy-start(f32[2,32]{1,0:T(2,128)} %param.25) | copy-start | bytes 772
  317.1 273.6 %copy-start.28 = (f32[2,32,1024]{2,1,0:T(8,128)S(1)}, f32[2,32,1024]{2,1,0:T(8,128)}, u32[]{:S(2)}) copy-start(f32[2,32,1024]{2,1,0:T(8,128)} %param.20) | copy-start | bytes 786436
  317.1 273.6 %copy-start.39 = (f32[2,32,1024]{2,1,0:T(8,128)S(1)}, f32[2,32,1024]{2,1,0:T(8,128)}, u32[]{:S(2)}) copy-start(f32[2,32,1024]{2,1,0:T(8,128)} %param.21) | copy-start | bytes 786436
  317.1 273.6 %copy-start.40 = (f32[2,32,1024]{2,1,0:T(8,128)S(1)}, f32[2,32,1024]{2,1,0:T(8,128)}, u32[]{:S(2)}) copy-start(f32[2,32,1024]{2,1,0:T(8,128)} %param.22) | copy-start | bytes 786436
  (26 other events, 67.8 us)
Sparse Core Ops, SparseCore 0:
  11.4 59.1 all-gather.5
  74.0 55.5 all-gather.7
  305.2 146.1 reduce-scatter.4
  453.5 137.1 reduce-scatter.2

commit v2 on v1

v2 whole, which is shorter than its diff:
```python
import functools

import jax
import jax.numpy as jnp
from jax import lax
from jax.experimental import pallas as pl
from jax.experimental.pallas import tpu as pltpu
from jax.sharding import PartitionSpec as P

PW = 32
STEPS = 4
TILE = 256

time_step = 0.15
learn_rate = 0.001
beta_one = 0.9
beta_two = 0.99
adam_count = 20
tiny_eps = 1e-08

MESH = pl.DeviceIdType.MESH
F32 = jnp.float32
BF16 = jnp.bfloat16


def adam(param, moment, second, grad):
    moment_new = beta_one * moment + (1.0 - beta_one) * grad
    second_new = beta_two * second + (1.0 - beta_two) * grad * grad
    mhat = moment_new / (1.0 - beta_one**adam_count)
    vhat = second_new / (1.0 - beta_two**adam_count)
    return (param - learn_rate * mhat / (jnp.sqrt(vhat) + tiny_eps), moment_new, second_new)


def dims_of(gx, gy):
    nx = max(1, gx // 4)
    return (gx // nx, nx, gy // 2, 2)


def kernel(
    gx_n,
    gy_n,
    field,
    cond,
    rate,
    cell,
    trainer,
    slot,
    store,
    w,
    wm,
    wv,
    bias,
    new_field,
    new_w,
    new_wm,
    new_wv,
    bias_grad,
    ua,
    ub,
    coef,
    cz,
    table,
    half,
    rows,
    counts,
    w0,
    w1,
    small,
    hid,
    hidb,
    gpb,
    g0,
    g1,
    brow,
    bsum,
    xsend,
    ysend,
    xrecv,
    yrecv,
    rc0,
    ra0,
    rb0,
    rz0,
    rc1,
    ra1,
    rb1,
    rz1,
    bbuf,
    half_sem,
    hs_sem,
    hr_sem,
    ag_s,
    ag_r,
    rs_s,
    rs_r,
    bs_s,
    bs_r,
):
    dims = dims_of(gx_n, gy_n)
    nz, nx, ny, nc = dims
    gx, gy = lax.axis_index("gx"), lax.axis_index("gy")
    here = (gx // nx, lax.rem(gx, nx), gy // nc, lax.rem(gy, nc))
    depth, cx, cy = field.shape
    width = w.shape[2]

    def device(axis, pos):
        p = list(here)
        p[axis] = pos
        return (p[0] * nx + p[1], p[2] * nc + p[3])

    barrier = pltpu.get_barrier_semaphore()
    for o in range(1, gx_n):
        pl.semaphore_signal(
            barrier, inc=1, device_id=(lax.rem(gx + o, gx_n), gy), device_id_type=MESH
        )
    for o in range(1, gy_n):
        pl.semaphore_signal(
            barrier, inc=1, device_id=(gx, lax.rem(gy + o, gy_n)), device_id_type=MESH
        )

    load = pltpu.make_async_copy(store.at[:, pl.ds(0, width)], half, half_sem.at[0])
    load.start()

    w0[here] = w[0].astype(w0.dtype)
    w1[here] = w[1].astype(w1.dtype)
    devices = gx_n * gy_n
    lane = lax.broadcasted_iota(jnp.int32, (trainer.shape[0], 128), 1)
    hot_t = (trainer[...] == lane).astype(F32)
    sm = jnp.concatenate([jnp.sum(hot_t, 0, keepdims=True), bias[1:8, :]], 0)
    small[here] = sm

    zero_x = jnp.zeros((depth, cy), F32)
    zero_y = jnp.zeros((cx, 128), F32)

    lanes = lax.broadcasted_iota(jnp.int32, (cx, cy), 1)
    subl = lax.broadcasted_iota(jnp.int32, (cx, cy), 0)

    def pack(index, plane):
        def one(z, acc):
            u = plane(z)
            xsend[index, 0, pl.ds(z, 1), :] = u[0:1, :]
            xsend[index, 1, pl.ds(z, 1), :] = u[cx - 1 : cx, :]
            acc = jnp.where(lanes == z, pltpu.roll(u, z, 1), acc)
            return jnp.where(
                lanes == depth + z, pltpu.roll(u, lax.rem(depth + z + 1, cy), 1), acc
            )

        ysend[index] = lax.fori_loop(0, depth, one, jnp.zeros((cx, cy), F32))

    def halo(index):
        out = []
        for side, (axis_pos, n, mk) in enumerate(
            (
                (gx, gx_n, lambda p: (p, gy)),
                (gx, gx_n, lambda p: (p, gy)),
                (gy, gy_n, lambda p: (gx, p)),
                (gy, gy_n, lambda p: (gx, p)),
            )
        ):
            up = side % 2 == 0
            sendbuf = (
                xsend.at[index, 1 if up else 0] if side < 2 else ysend.at[index]
            )
            recvbuf = (xrecv if side < 2 else yrecv).at[index, 0 if up else 1]
            peer = jnp.minimum(axis_pos + 1, n - 1) if up else jnp.maximum(axis_pos - 1, 0)
            copy = pltpu.make_async_remote_copy(
                src_ref=sendbuf,
                dst_ref=recvbuf,
                send_sem=hs_sem.at[index, side],
                recv_sem=hr_sem.at[index, side],
                device_id=mk(peer),
                device_id_type=MESH,
            )
            sends = axis_pos < n - 1 if up else axis_pos > 0
            gets = axis_pos > 0 if up else axis_pos < n - 1
            out.append((copy, sends, gets))
        return out

    def halo_start(index):
        for copy, sends, gets in halo(index):
            pl.when(sends)(copy.start)

    def halo_wait(index):
        for side, (copy, sends, gets) in enumerate(halo(index)):
            pl.when(sends)(copy.wait_send)
            pl.when(gets)(copy.wait_recv)
            buf = xrecv if side < 2 else yrecv

            @pl.when(jnp.logical_not(gets))
            def _():
                buf[index, side % 2] = zero_x if side < 2 else zero_y

    def region(done, fixed=None):
        ind = []
        for a in range(4):
            if fixed is not None and a == fixed[0]:
                ind.append(fixed[1])
            else:
                ind.append(slice(None) if a in done else here[a])
        return tuple(ind)

    def gather(buf, order, which):
        done = []
        for phase, axis in enumerate(order):
            n = dims[axis]
            copies = []
            for o in range(1, n):
                ref = buf.at[region(done)]
                copy = pltpu.make_async_remote_copy(
                    src_ref=ref,
                    dst_ref=ref,
                    send_sem=ag_s.at[which, axis, o - 1],
                    recv_sem=ag_r.at[which, axis, o - 1],
                    device_id=device(axis, lax.rem(here[axis] + o, n)),
                    device_id_type=MESH,
                )
                copy.start()
                copies.append(copy)
            yield
            for copy in copies:
                copy.wait()
            done.append(axis)
            yield

    def step(gens):
        for g in gens:
            next(g, None)

    pack(0, lambda z: cond[z])
    pack(1, lambda z: field[z])
    pl.semaphore_wait(barrier, gx_n - 1 + gy_n - 1)
    halo_start(0)
    halo_start(1)
    gens = [
        gather(small, (0, 1, 2, 3), 0),
        gather(w0, (0, 1, 2, 3), 1),
        gather(w1, (0, 2, 1, 3), 2),
    ]
    step(gens)

    n_old = slot.shape[0]
    n_slots = store.shape[0]

    def pick(col):
        def one(t, carry):
            r = pl.ds(pl.multiple_of(t * TILE, TILE), TILE)
            hot = (
                slot[r, :] == lax.broadcasted_iota(jnp.int32, (TILE, n_slots), 1)
            ).astype(F32).astype(BF16)
            rows[r, pl.ds(col, width)] = jnp.dot(
                hot, half[...], preferred_element_type=F32
            ).astype(BF16)
            return carry

        lax.fori_loop(0, n_old // TILE, one, 0)

    def shifted(u, index, z):
        lo = xrecv[index, 0, pl.ds(z, 1), :]
        hi = xrecv[index, 1, pl.ds(z, 1), :]
        xm = jnp.where(subl == 0, lo, pltpu.roll(u, 1, 0))
        xp = jnp.where(subl == cx - 1, hi, pltpu.roll(u, cx - 1, 0))
        left = pltpu.roll(yrecv[index, 0], lax.rem(2 * cy - depth - z, cy), 1)
        right = pltpu.roll(yrecv[index, 1], cy - 1 - z, 1)
        ym = jnp.where(lanes == 0, left, pltpu.roll(u, 1, 1))
        yp = jnp.where(lanes == cy - 1, right, pltpu.roll(u, cy - 1, 1))
        return xm, xp, ym, yp

    half_step = 0.5 * time_step
    for buf in (ua, ub):
        buf[0] = jnp.zeros((cx, cy), F32)
        buf[depth + 1] = jnp.zeros((cx, cy), F32)
    cz[0] = half_step * cond[0]
    cz[depth] = half_step * cond[depth - 1]

    def z_coef(z, carry):
        cz[z] = half_step * (cond[z - 1] + cond[z])
        return carry

    lax.fori_loop(1, depth, z_coef, 0)
    halo_wait(0)

    def make_coef(z, carry):
        k = cond[z]
        total = time_step * rate[z] + cz[z] + cz[z + 1]
        for i, kn in enumerate(shifted(k, 0, z)):
            c = half_step * (k + kn)
            coef[i, z] = c
            total = total + c
        coef[4, z] = 1.0 - total
        ua[z + 1] = field[z]
        return carry

    lax.fori_loop(0, depth, make_coef, 0)

    def advance(index, src, dst):
        def one(z, carry):
            u = src[z + 1]
            acc = coef[4, z] * u + cz[z] * src[z] + cz[z + 1] * src[z + 2]
            for i, un in enumerate(shifted(u, index, z)):
                acc = acc + coef[i, z] * un
            dst[z + 1] = acc
            return carry

        lax.fori_loop(0, depth, one, 0)

    load.wait()
    pick(0)
    load2 = pltpu.make_async_copy(store.at[:, pl.ds(width, width)], half, half_sem.at[1])
    load2.start()
    step(gens)
    step(gens)

    halo_wait(1)
    bufs = (ua, ub)
    for s in range(STEPS):
        src, dst = bufs[s % 2], bufs[(s + 1) % 2]
        advance(s + 1, src, dst)
        if s < STEPS - 1:
            pack(s + 2, lambda z: dst[z + 1])
            halo_start(s + 2)
            if s == 0:
                load2.wait()
                pick(width)
            if s == 1:
                step(gens)
                step(gens)
            halo_wait(s + 2)
    last = bufs[STEPS % 2]

    blocks = cy // PW
    per = 128 // PW
    group = lanes // PW

    def build(offset, plane):
        def one(q, carry):
            planes = [plane(q * per + j) for j in range(per)]
            for b in range(blocks):
                acc = None
                for j in range(per):
                    shift = (PW * (j - b)) % cy
                    v = planes[j] if shift == 0 else pltpu.roll(planes[j], shift, 1)
                    acc = v if acc is None else jnp.where(group == j, v, acc)
                table[
                    b * cx : (b + 1) * cx,
                    pl.ds(pl.multiple_of(offset + q * 128, 128), 128),
                ] = acc.astype(BF16)
            return carry

        lax.fori_loop(0, depth // per, one, 0)

    build(0, lambda z: field[z])
    build(width, lambda z: last[z + 1])

    def emit(z, carry):
        new_field[z] = last[z + 1]
        return carry

    lax.fori_loop(0, depth, emit, 0)
    n_new = cell.shape[0]
    n_cells = table.shape[0]
    hot_c = (
        (cell[...] == lax.broadcasted_iota(jnp.int32, (n_new, n_cells), 1))
        .astype(F32)
        .astype(BF16)
    )
    for c in range(0, 2 * width, 512):
        rows[n_old : n_old + n_new, c : c + 512] = jnp.dot(
            hot_c, table[:, c : c + 512], preferred_element_type=F32
        ).astype(BF16)

    step(gens)
    step(gens)
    step(gens)

    everyone = small[...].reshape(devices, 8, 128)
    totals = jnp.sum(everyone[:, 0, :], 0, keepdims=True) + float(n_old)
    position = gx * gy_n + gy
    lane1 = lax.broadcasted_iota(jnp.int32, (1, 128), 1)
    mine = jnp.sum(jnp.where(lane1 == position, totals, 0.0), 1, keepdims=True)
    counts[0:n_old, :] = jnp.broadcast_to(mine, (n_old, 128))
    counts[n_old : n_old + n_new, :] = jnp.broadcast_to(
        jnp.sum(hot_t * totals, 1, keepdims=True), (n_new, 128)
    )
    share = width // devices
    fit = 128 // share
    for layer in range(2):
        for j in range(width // 128):
            acc = jnp.zeros((1, 128), F32)
            for i in range(fit):
                acc = jnp.where(lane1 // share == i, everyone[j * fit + i, layer + 1 : layer + 2, :], acc)
            brow[layer : layer + 1, j * 128 : (j + 1) * 128] = acc.astype(BF16).astype(F32)

    n_rows = n_old + n_new
    bsum[...] = jnp.zeros_like(bsum)

    def whole(ref):
        return ref[...].astype(BF16).reshape(width, width)

    def forward(t, carry):
        r = pl.ds(pl.multiple_of(t * TILE, TILE), TILE)
        pre = jnp.dot(rows[r, :width], whole(w0), preferred_element_type=F32) + brow[0:1, :]
        h = jnp.tanh(pre)
        hid[r, :] = h
        hidb[r, :] = h.astype(BF16)
        return carry

    lax.fori_loop(0, n_rows // TILE, forward, 0)

    def forward2(t, carry):
        r = pl.ds(pl.multiple_of(t * TILE, TILE), TILE)
        pred = jnp.dot(hidb[r, :], whole(w1), preferred_element_type=F32) + brow[1:2, :]
        gp = 2.0 * (pred - rows[r, width : 2 * width].astype(F32)) / counts[r, 0:1]
        gpb[r, :] = gp.astype(BF16)
        bsum[1:2, :] += jnp.sum(gp, 0, keepdims=True)
        return carry

    lax.fori_loop(0, n_rows // TILE, forward2, 0)

    def reduce(buf, order, stages, which):
        left = [0, 1, 2, 3]
        for phase, axis in enumerate(order):
            n = dims[axis]
            stage = stages[phase]
            copies = []
            for o in range(1, n):
                peer = lax.rem(here[axis] + o, n)
                copy = pltpu.make_async_remote_copy(
                    src_ref=buf.at[region(left, (axis, peer))],
                    dst_ref=stage.at[o - 1],
                    send_sem=rs_s.at[which, axis, o - 1],
                    recv_sem=rs_r.at[which, axis, o - 1],
                    device_id=device(axis, peer),
                    device_id_type=MESH,
                )
                copy.start()
                copies.append(copy)
            yield
            left.remove(axis)
            own = region(left)
            for o, copy in enumerate(copies):
                copy.wait()
            shape = [dims[a] for a in range(4) if a in left]

            def total(i, carry):
                ind, sub, rest = [], [], i
                for a in reversed(left):
                    ind.insert(0, lax.rem(rest, dims[a]))
                    rest = rest // dims[a]
                full = list(here)
                for a, v in zip(left, ind):
                    full[a] = v
                acc = buf[tuple(full)]
                for o in range(n - 1):
                    acc = acc + stage[(o, *ind)]
                buf[tuple(full)] = acc
                return carry

            count = 1
            for m in shape:
                count *= m
            if count == 1:
                total(0, 0)
            else:
                lax.fori_loop(0, count, total, 0)
            yield

    def reduce_bias():
        for phase, axis in enumerate((3, 2, 1, 0)):
            n = dims[axis]
            copies = []
            for o in range(1, n):
                copy = pltpu.make_async_remote_copy(
                    src_ref=bbuf.at[axis, 0],
                    dst_ref=bbuf.at[axis, o],
                    send_sem=bs_s.at[axis, o - 1],
                    recv_sem=bs_r.at[axis, o - 1],
                    device_id=device(axis, lax.rem(here[axis] + o, n)),
                    device_id_type=MESH,
                )
                copy.start()
                copies.append(copy)
            yield
            for copy in copies:
                copy.wait()
            acc = bbuf[axis, 0]
            for o in range(1, n):
                acc = acc + bbuf[axis, o]
            if axis > 0:
                bbuf[axis - 1, 0] = acc
            else:
                bias_grad[...] = acc
            yield

    across = (((0,), (0,)), ((), ()))

    def store_grad(buf, col, value):
        per_tile = TILE // share
        flat = value.reshape(per_tile, share, width)

        for i in range(per_tile):
            d = col * per_tile + i
            buf[
                d // (nx * ny * nc),
                lax.rem(d // (ny * nc), nx),
                lax.rem(d // nc, ny),
                lax.rem(d, nc),
            ] = flat[i]

    def grad_two(j, carry):
        c = pl.ds(pl.multiple_of(j * TILE, TILE), TILE)
        store_grad(
            g1, j, lax.dot_general(hidb[:, c], gpb[...], across, preferred_element_type=F32)
        )
        return carry

    lax.fori_loop(0, width // TILE, grad_two, 0)
    red1 = reduce(g1, (3, 1, 2, 0), (rc1, ra1, rb1, rz1), 1)
    next(red1)

    def backward(t, carry):
        r = pl.ds(pl.multiple_of(t * TILE, TILE), TILE)
        gh = lax.dot_general(
            gpb[r, :], whole(w1), (((1,), (1,)), ((), ())), preferred_element_type=F32
        )
        h = hid[r, :]
        ga = gh * (1.0 - h * h)
        hidb[r, :] = ga.astype(BF16)
        bsum[0:1, :] += jnp.sum(ga, 0, keepdims=True)
        return carry

    lax.fori_loop(0, n_rows // TILE, backward, 0)
    bbuf[3, 0] = bsum[...]
    redb = reduce_bias()
    next(redb)
    next(red1)
    next(red1)

    def grad_one(j, carry):
        c = pl.ds(pl.multiple_of(j * TILE, TILE), TILE)
        store_grad(
            g0, j, lax.dot_general(rows[:, c], hidb[...], across, preferred_element_type=F32)
        )
        return carry

    lax.fori_loop(0, width // TILE, grad_one, 0)
    red0 = reduce(g0, (3, 2, 1, 0), (rc0, rb0, ra0, rz0), 0)
    next(red0)
    for _ in range(2):
        next(redb, None)
    for _ in range(3):
        step([red0, red0])
        step([red1, red1])
        step([redb, redb])

    def finish(layer, buf):
        p, m, v = adam(w[layer], wm[layer], wv[layer], buf[here])
        new_w[layer] = p
        new_wm[layer] = m
        new_wv[layer] = v

    step([red1])
    finish(1, g1)
    step([red0])
    finish(0, g0)
    step([redb, redb])


def local(
    field,
    conductivity,
    rate,
    patch_cell,
    trainer,
    res_slot,
    reservoir,
    weights,
    w_mom,
    w_var,
    biases,
    b_mom,
    b_var,
):
    gx_n, gy_n = lax.axis_size("gx"), lax.axis_size("gy")
    devices = gx_n * gy_n
    dims = dims_of(gx_n, gy_n)
    nz, nx, ny, nc = dims
    depth, cx, cy = field.shape
    share, width = weights.shape[1], weights.shape[2]
    blocks = cy // PW
    n_old, n_new = res_slot.shape[0], patch_cell.shape[0]
    n_rows = n_old + n_new
    cell = ((patch_cell % blocks) * cx + patch_cell // blocks)[:, None]
    slot = res_slot[:, None]
    wide = jnp.tile(biases, (1, 128 // share))
    bias8 = jnp.concatenate([jnp.zeros((1, 128), F32), wide, jnp.zeros((5, 128), F32)], 0)
    wire = BF16 if share % 16 == 0 else F32
    most = max(dims) - 1
    full = (*dims, share, width)
    vm = pl.BlockSpec(memory_space=pltpu.VMEM)
    shard = jax.ShapeDtypeStruct(weights.shape, F32)

    def scratch(*shape, dtype=F32):
        return pltpu.VMEM(shape, dtype)

    dma = pltpu.SemaphoreType.DMA
    out = pl.pallas_call(
        functools.partial(kernel, gx_n, gy_n),
        out_shape=(
            jax.ShapeDtypeStruct(field.shape, F32),
            shard,
            shard,
            shard,
            jax.ShapeDtypeStruct((8, width), F32),
        ),
        in_specs=[vm] * 6 + [pl.BlockSpec(memory_space=pl.ANY)] + [vm] * 4,
        out_specs=[vm] * 5,
        scratch_shapes=[
            scratch(depth + 2, cx, cy),
            scratch(depth + 2, cx, cy),
            scratch(5, depth, cx, cy),
            scratch(depth + 1, cx, cy),
            scratch(blocks * cx, 2 * width, dtype=BF16),
            scratch(reservoir.shape[0], width, dtype=BF16),
            scratch(n_rows, 2 * width, dtype=BF16),
            scratch(n_rows, 128),
            scratch(*full, dtype=wire),
            scratch(*full, dtype=wire),
            scratch(*dims, 8, 128),
            scratch(n_rows, width),
            scratch(n_rows, width, dtype=BF16),
            scratch(n_rows, width, dtype=BF16),
            scratch(*full),
            scratch(*full),
            scratch(8, width),
            scratch(8, width),
            scratch(STEPS + 1, 2, depth, cy),
            scratch(STEPS + 1, cx, cy),
            scratch(STEPS + 1, 2, depth, cy),
            scratch(STEPS + 1, 2, cx, cy),
            scratch(nc - 1, nz, nx, ny, share, width),
            scratch(nx - 1, nz, share, width),
            scratch(ny - 1, nz, nx, share, width),
            scratch(nz - 1, share, width),
            scratch(nc - 1, nz, nx, ny, share, width),
            scratch(nx - 1, nz, ny, share, width),
            scratch(ny - 1, nz, share, width),
            scratch(nz - 1, share, width),
            scratch(4, most + 1, 8, width),
            dma((2,)),
            dma((STEPS + 1, 4)),
            dma((STEPS + 1, 4)),
            dma((3, 4, most)),
            dma((3, 4, most)),
            dma((2, 4, most)),
            dma((2, 4, most)),
            dma((4, most)),
            dma((4, most)),
        ],
        compiler_params=pltpu.CompilerParams(
            collective_id=0, has_side_effects=True, vmem_limit_bytes=62 * 2**20
        ),
        cost_estimate=pl.CostEstimate(
            flops=10 * n_rows * width * width, bytes_accessed=32 * 2**20, transcendentals=0
        ),
    )(field, conductivity, rate, cell, trainer, slot, reservoir, weights, w_mom, w_var, bias8)
    state, new_w, new_wm, new_wv, bias_grad = out
    position = lax.axis_index("gx") * gy_n + lax.axis_index("gy")
    share_b = lax.dynamic_slice_in_dim(bias_grad[:2], position * share, share, 1)
    new_b, new_bm, new_bv = adam(biases, b_mom, b_var, share_b)
    return (state, new_w, new_wm, new_wv, new_b, new_bm, new_bv)


def solution(mesh):
    return jax.shard_map(
        local,
        mesh=mesh,
        in_specs=(
            P(None, "gx", "gy"),
            P(None, "gx", "gy"),
            P(None, "gx", "gy"),
            P(("gx", "gy")),
            P(("gx", "gy"), None),
            P(("gx", "gy")),
            P(("gx", "gy"), None),
            P(None, ("gx", "gy"), None),
            P(None, ("gx", "gy"), None),
            P(None, ("gx", "gy"), None),
            P(None, ("gx", "gy")),
            P(None, ("gx", "gy")),
            P(None, ("gx", "gy")),
        ),
        out_specs=(
            P(None, "gx", "gy"),
            P(None, ("gx", "gy"), None),
            P(None, ("gx", "gy"), None),
            P(None, ("gx", "gy"), None),
            P(None, ("gx", "gy")),
            P(None, ("gx", "gy")),
            P(None, ("gx", "gy")),
        ),
        check_vma=False,
    )
```

time: 609 us -> 169 us (0.28); the launches traced: 600 us -> 168 us
  waiting for transfers between devices: 229 us -> 0 us
  Pallas kernels: 0 us -> 153 us
  blocking collectives: 126 us -> 0 us
  local copies, waits for them, and re-layouts: 90.1 us -> 12.9 us
  starting transfers between devices: 53.3 us -> 0 us
  other arithmetic: 54.6 us -> 2.02 us
  matrix products: 31.1 us -> 0 us
  between operations: 15.1 us -> 0.66 us
    reduce_scatter x2 -> x0, waiting for transfers between devices: 227 us -> none  [local(): lax.psum_scatter(g, axes, scatter_dimension=0, tiled=True)]
    pallas_call x0 -> x1, Pallas kernels: none -> 153 us  [local(): pl.pallas_call(functools.partial(kernel, gx_n, gy_n), out_shape=(jax.Shap...]
    psum x2 -> x0, blocking collectives: 86.8 us -> none  [the longest x1 46 us: local(): whole_b = lax.psum(grad_b, axes)]
    ppermute x20 -> x0, starting transfers between devices: 53.1 us -> none  [the longest x10 39.8 us: with_halo(): before = lax.ppermute(last, axis, up)]
    all_gather x1 -> x0, blocking collectives: 39.2 us -> none  [local(): bbf = lax.all_gather(biases.astype(jnp.bfloat16), axes, axis=1, tiled=True)]
    dot_general x5 -> x0, matrix products: 31.1 us -> none  [the longest x1 7.45 us: local_grads(): jnp.dot(inputs, wbf[0], preferred_element_type=jnp.float32)]
    slice x21 -> x1, local copies, waits for them, and re-layouts: 27.3 us -> 0.76 us  [local(): bias_grad[:2]]
    gather x3 -> x0, local copies, waits for them, and re-layouts: 24.1 us -> none  [the longest x1 13.4 us: local(): rows = jnp.concatenate([reservoir[res_slot], patches], 0)]
  transfers between devices with their start and end apart: 24 -> 0, of which waited for: 5 -> 0; matrix products, arithmetic and copies ran while one was open for 26% -> 0% of each run, Pallas kernels for 0% -> 0%
where the time goes in v2:
time: 169 us; the launch traced here: 168 us
  Pallas kernels  153 us (91%)
  local copies, waits for them, and re-layouts  12.9 us (8%)
  other arithmetic  2.02 us (1%)
    pallas_call x1, Pallas kernels, local(): pl.pallas_call(functools.partial(kernel, gx_n, gy_n), out_shape=(jax.Shap...  153 us
    unnamed x11, local copies, waits for them, and re-layouts  8.8 us

profile of v2, /device:TPU:0, one launch (start us, length us, event | category | flops | bytes accessed | tf_op | source)
XLA Modules:
  0.0 168.4 jit_solution(15729474552783473100)
XLA Ops:
  0.6 1.7 %copy.23.slot = s32[1024,1]{1,0:T(8,128)} copy(s32[1024,1]{0,1:T(1,128)} %bitcast.3) | data formatting | bytes 8192 | tf_op jit(solution)/shard_map/broadcast_in_dim | solution.py:593
  2.3 0.7 fusion.2
  3.0 0.8 copy.21.cell
  3.8 1.5 copy.22.trainer
  5.3 0.7 tile.4
  6.0 0.1 tile.10
  6.1 0.1 pad.2.clone
  6.2 0.7 maximum_maximum_fusion.bias
  6.8 0.0 copy-start
  6.8 0.0 copy-start.1
  6.8 0.0 copy-start.2
  6.8 152.8 %shard_map.180 = (f32[32,64,128]{2,1,0:T(8,128)}, f32[2,32,1024]{2,1,0:T(8,128)}, f32[2,32,1024]{2,1,0:T(8,128)}, f32[2,32,1024]{2,1,0:T(8,128)}, f32[8,1024]{1,0:T(8,128)}) custom-call(f32[32,64,128]{2,1,0:T(8,128)} %field.1, f32[32,64,128]{2,1,0:T(8,128)} %cond.1, f32[32,64,128]{2,1,0:T(8,128)} %rate.1, s32[256,1]{1,0:T(8,128)} %copy.21.cell, ...), custom_call_target="tpu_custom_call" | custom-call | flops 13421772800 | bytes 33554432 | tf_op jit(solution)/shard_map/pallas_call | solution.py:606
  159.7 0.8 slice.3
  160.4 0.0 copy-done
  160.4 0.0 copy-done.1
  160.4 0.0 copy-done.2
  160.4 0.7 divide_subtract_fusion
  161.1 2.3 %copy.28 = f32[32,64,128]{2,1,0:T(8,128)} copy(f32[32,64,128]{2,1,0:T(8,128)} %get-tuple-element.27) | data formatting | bytes 2097152
  163.4 1.7 copy.29
  165.1 1.7 copy.30
  166.7 1.7 copy.31
  (2 shorter events, 0.0 us)
Async XLA Ops:
  6.8 153.6 %copy-start = (f32[2,32]{1,0:T(2,128)S(1)}, f32[2,32]{1,0:T(2,128)}, u32[]{:S(2)}) copy-start(f32[2,32]{1,0:T(2,128)} %param.23) | copy-start | bytes 772
  6.8 153.6 %copy-start.1 = (f32[2,32]{1,0:T(2,128)S(1)}, f32[2,32]{1,0:T(2,128)}, u32[]{:S(2)}) copy-start(f32[2,32]{1,0:T(2,128)} %param.24) | copy-start | bytes 772
  6.8 153.6 %copy-start.2 = (f32[2,32]{1,0:T(2,128)S(1)}, f32[2,32]{1,0:T(2,128)}, u32[]{:S(2)}) copy-start(f32[2,32]{1,0:T(2,128)} %param.25) | copy-start | bytes 772

commit v3 on v2

--- a/solution.py
+++ b/solution.py
@@ -42,19 +42,17 @@
     field,
     cond,
     rate,
+    ids,
+    store,
+    w,
+    bias,
+    new_field,
+    grad_out,
+    bias_grad,
+    slot,
     cell,
     trainer,
-    slot,
-    store,
-    w,
-    wm,
-    wv,
-    bias,
-    new_field,
-    new_w,
-    new_wm,
-    new_wv,
-    bias_grad,
+    tiny,
     ua,
     ub,
     coef,
@@ -67,7 +65,6 @@
     w1,
     small,
     hid,
-    hidb,
     gpb,
     g0,
     g1,
@@ -77,14 +74,8 @@
     ysend,
     xrecv,
     yrecv,
-    rc0,
-    ra0,
-    rb0,
-    rz0,
-    rc1,
-    ra1,
-    rb1,
-    rz1,
+    stages0,
+    stages1,
     bbuf,
     half_sem,
     hs_sem,
@@ -102,6 +93,15 @@
     here = (gx // nx, lax.rem(gx, nx), gy // nc, lax.rem(gy, nc))
     depth, cx, cy = field.shape
     width = w.shape[2]
+    hidb = half.at[pl.ds(0, rows.shape[0])]
+
+    def loop(count, body, together):
+        def several(q, carry):
+            for j in range(together):
+                body(q * together + j)
+            return carry
+
+        lax.fori_loop(0, count // together, several, 0)
 
     def device(axis, pos):
         p = list(here)
@@ -124,10 +124,24 @@
     w0[here] = w[0].astype(w0.dtype)
     w1[here] = w[1].astype(w1.dtype)
     devices = gx_n * gy_n
-    lane = lax.broadcasted_iota(jnp.int32, (trainer.shape[0], 128), 1)
+    share = w.shape[1]
+    upright = jnp.transpose(ids[...])
+    place = 0
+    for ref in (slot, cell, trainer):
+        for g in range(ref.shape[0] // 128):
+            ref[g * 128 : (g + 1) * 128, :] = jnp.broadcast_to(
+                upright[:, place : place + 1], (128, 128)
+            )
+            place += 1
+    lane = lax.broadcasted_iota(jnp.int32, trainer.shape, 1)
     hot_t = (trainer[...] == lane).astype(F32)
-    sm = jnp.concatenate([jnp.sum(hot_t, 0, keepdims=True), bias[1:8, :]], 0)
+    tiny[...] = jnp.zeros_like(tiny)
+    tiny[1:3, 0:share] = bias[...]
+    sm = tiny[...]
+    for i in range(1, 128 // share):
+        sm = sm + pltpu.roll(tiny[...], share * i, 1)
     small[here] = sm
+    small[(*here, pl.ds(0, 1))] = jnp.sum(hot_t, 0, keepdims=True)
 
     zero_x = jnp.zeros((depth, cy), F32)
     zero_y = jnp.zeros((cx, 128), F32)
@@ -136,16 +150,19 @@
     subl = lax.broadcasted_iota(jnp.int32, (cx, cy), 0)
 
     def pack(index, plane):
-        def one(z, acc):
-            u = plane(z)
-            xsend[index, 0, pl.ds(z, 1), :] = u[0:1, :]
-            xsend[index, 1, pl.ds(z, 1), :] = u[cx - 1 : cx, :]
-            acc = jnp.where(lanes == z, pltpu.roll(u, z, 1), acc)
-            return jnp.where(
-                lanes == depth + z, pltpu.roll(u, lax.rem(depth + z + 1, cy), 1), acc
-            )
-
-        ysend[index] = lax.fori_loop(0, depth, one, jnp.zeros((cx, cy), F32))
+        def several(q, acc):
+            for j in range(8):
+                z = q * 8 + j
+                u = plane(z)
+                xsend[index, 0, pl.ds(z, 1), :] = u[0:1, :]
+                xsend[index, 1, pl.ds(z, 1), :] = u[cx - 1 : cx, :]
+                acc = jnp.where(lanes == z, pltpu.roll(u, z, 1), acc)
+                acc = jnp.where(
+                    lanes == depth + z, pltpu.roll(u, lax.rem(depth + z + 1, cy), 1), acc
+                )
+            return acc
+
+        ysend[index] = lax.fori_loop(0, depth // 8, several, jnp.zeros((cx, cy), F32))
 
     def halo(index):
         out = []
@@ -226,33 +243,34 @@
         for g in gens:
             next(g, None)
 
-    pack(0, lambda z: cond[z])
-    pack(1, lambda z: field[z])
     pl.semaphore_wait(barrier, gx_n - 1 + gy_n - 1)
-    halo_start(0)
-    halo_start(1)
     gens = [
         gather(small, (0, 1, 2, 3), 0),
         gather(w0, (0, 1, 2, 3), 1),
         gather(w1, (0, 2, 1, 3), 2),
     ]
     step(gens)
+    pack(0, lambda z: cond[z])
+    halo_start(0)
+    pack(1, lambda z: field[z])
+    halo_start(1)
 
     n_old = slot.shape[0]
     n_slots = store.shape[0]
 
-    def pick(col):
+    def pick(col, first, last):
         def one(t, carry):
             r = pl.ds(pl.multiple_of(t * TILE, TILE), TILE)
             hot = (
-                slot[r, :] == lax.broadcasted_iota(jnp.int32, (TILE, n_slots), 1)
+                slot[r, 0:1] == lax.broadcasted_iota(jnp.int32, (TILE, n_slots), 1)
             ).astype(F32).astype(BF16)
             rows[r, pl.ds(col, width)] = jnp.dot(
                 hot, half[...], preferred_element_type=F32
             ).astype(BF16)
             return carry
 
-        lax.fori_loop(0, n_old // TILE, one, 0)
+        tiles = n_old // TILE
+        lax.fori_loop(tiles * first // 2, tiles * last // 2, one, 0)
 
     def shifted(u, index, z):
         lo = xrecv[index, 0, pl.ds(z, 1), :]
@@ -272,14 +290,17 @@
     cz[0] = half_step * cond[0]
     cz[depth] = half_step * cond[depth - 1]
 
-    def z_coef(z, carry):
+    def z_coef(z):
         cz[z] = half_step * (cond[z - 1] + cond[z])
-        return carry
-
-    lax.fori_loop(1, depth, z_coef, 0)
+        ua[z] = field[z - 1]
+
+    loop(depth - 1, lambda z: z_coef(z + 1), 1)
+    ua[depth] = field[depth - 1]
+    load.wait()
+    pick(0, 0, 1)
     halo_wait(0)
 
-    def make_coef(z, carry):
+    def make_coef(z):
         k = cond[z]
         total = time_step * rate[z] + cz[z] + cz[z + 1]
         for i, kn in enumerate(shifted(k, 0, z)):
@@ -287,45 +308,24 @@
             coef[i, z] = c
             total = total + c
         coef[4, z] = 1.0 - total
-        ua[z + 1] = field[z]
-        return carry
-
-    lax.fori_loop(0, depth, make_coef, 0)
+
+    loop(depth, make_coef, 4)
 
     def advance(index, src, dst):
-        def one(z, carry):
+        def one(z):
             u = src[z + 1]
             acc = coef[4, z] * u + cz[z] * src[z] + cz[z + 1] * src[z + 2]
             for i, un in enumerate(shifted(u, index, z)):
                 acc = acc + coef[i, z] * un
             dst[z + 1] = acc
-            return carry
-
-        lax.fori_loop(0, depth, one, 0)
-
-    load.wait()
-    pick(0)
+
+        loop(depth, one, 4)
+
+    pick(0, 1, 2)
     load2 = pltpu.make_async_copy(store.at[:, pl.ds(width, width)], half, half_sem.at[1])
     load2.start()
     step(gens)
     step(gens)
-
-    halo_wait(1)
-    bufs = (ua, ub)
-    for s in range(STEPS):
-        src, dst = bufs[s % 2], bufs[(s + 1) % 2]
-        advance(s + 1, src, dst)
-        if s < STEPS - 1:
-            pack(s + 2, lambda z: dst[z + 1])
-            halo_start(s + 2)
-            if s == 0:
-                load2.wait()
-                pick(width)
-            if s == 1:
-                step(gens)
-                step(gens)
-            halo_wait(s + 2)
-    last = bufs[STEPS % 2]
 
     blocks = cy // PW
     per = 128 // PW
@@ -348,18 +348,36 @@
 
         lax.fori_loop(0, depth // per, one, 0)
 
-    build(0, lambda z: field[z])
+    halo_wait(1)
+    bufs = (ua, ub)
+    for s in range(STEPS):
+        src, dst = bufs[s % 2], bufs[(s + 1) % 2]
+        advance(s + 1, src, dst)
+        if s < STEPS - 1:
+            pack(s + 2, lambda z: dst[z + 1])
+            halo_start(s + 2)
+            if s == 0:
+                load2.wait()
+                pick(width, 0, 1)
+            if s == 1:
+                pick(width, 1, 2)
+                step(gens)
+                step(gens)
+            if s == 2:
+                build(0, lambda z: field[z])
+            halo_wait(s + 2)
+    last = bufs[STEPS % 2]
+
     build(width, lambda z: last[z + 1])
 
-    def emit(z, carry):
+    def emit(z):
         new_field[z] = last[z + 1]
-        return carry
-
-    lax.fori_loop(0, depth, emit, 0)
+
+    loop(depth, emit, 4)
     n_new = cell.shape[0]
     n_cells = table.shape[0]
     hot_c = (
-        (cell[...] == lax.broadcasted_iota(jnp.int32, (n_new, n_cells), 1))
+        (cell[:, 0:1] == lax.broadcasted_iota(jnp.int32, (n_new, n_cells), 1))
         .astype(F32)
         .astype(BF16)
     )
@@ -381,7 +399,6 @@
     counts[n_old : n_old + n_new, :] = jnp.broadcast_to(
         jnp.sum(hot_t * totals, 1, keepdims=True), (n_new, 128)
     )
-    share = width // devices
     fit = 128 // share
     for layer in range(2):
         for j in range(width // 128):
@@ -391,77 +408,107 @@
             brow[layer : layer + 1, j * 128 : (j + 1) * 128] = acc.astype(BF16).astype(F32)
 
     n_rows = n_old + n_new
+    tall = 640 if n_rows % 640 == 0 else TILE
     bsum[...] = jnp.zeros_like(bsum)
 
     def whole(ref):
         return ref[...].astype(BF16).reshape(width, width)
 
     def forward(t, carry):
-        r = pl.ds(pl.multiple_of(t * TILE, TILE), TILE)
+        r = pl.ds(pl.multiple_of(t * tall, tall), tall)
         pre = jnp.dot(rows[r, :width], whole(w0), preferred_element_type=F32) + brow[0:1, :]
         h = jnp.tanh(pre)
         hid[r, :] = h
         hidb[r, :] = h.astype(BF16)
         return carry
 
-    lax.fori_loop(0, n_rows // TILE, forward, 0)
+    lax.fori_loop(0, n_rows // tall, forward, 0)
 
     def forward2(t, carry):
-        r = pl.ds(pl.multiple_of(t * TILE, TILE), TILE)
+        r = pl.ds(pl.multiple_of(t * tall, tall), tall)
         pred = jnp.dot(hidb[r, :], whole(w1), preferred_element_type=F32) + brow[1:2, :]
         gp = 2.0 * (pred - rows[r, width : 2 * width].astype(F32)) / counts[r, 0:1]
         gpb[r, :] = gp.astype(BF16)
         bsum[1:2, :] += jnp.sum(gp, 0, keepdims=True)
         return carry
 
-    lax.fori_loop(0, n_rows // TILE, forward2, 0)
+    lax.fori_loop(0, n_rows // tall, forward2, 0)
+
+    coded = share % 16 == 0
+
+    def each(left, body):
+        count = 1
+        for a in left:
+            count *= dims[a]
+
+        def one(i, carry):
+            ind, rest = [], i
+            for a in reversed(left):
+                ind.insert(0, lax.rem(rest, dims[a]))
+                rest = rest // dims[a]
+            full = list(here)
+            for a, v in zip(left, ind):
+                full[a] = v
+            body(full, ind)
+            return carry
+
+        if count == 1:
+            one(0, 0)
+        else:
+            lax.fori_loop(0, count, one, 0)
 
     def reduce(buf, order, stages, which):
         left = [0, 1, 2, 3]
         for phase, axis in enumerate(order):
             n = dims[axis]
-            stage = stages[phase]
+            others = [a for a in left if a != axis]
+            out, got, out_scale, got_scale = stages[phase]
             copies = []
             for o in range(1, n):
                 peer = lax.rem(here[axis] + o, n)
-                copy = pltpu.make_async_remote_copy(
-                    src_ref=buf.at[region(left, (axis, peer))],
-                    dst_ref=stage.at[o - 1],
-                    send_sem=rs_s.at[which, axis, o - 1],
-                    recv_sem=rs_r.at[which, axis, o - 1],
-                    device_id=device(axis, peer),
-                    device_id_type=MESH,
-                )
-                copy.start()
-                copies.append(copy)
+                pairs = [(buf.at[region(left, (axis, peer))], got.at[o - 1])]
+                if coded:
+
+                    def encode(full, ind):
+                        full[axis] = peer
+                        v = buf[tuple(full)]
+                        top = jnp.max(jnp.abs(v), axis=0, keepdims=True)
+                        top = jnp.maximum(jnp.max(top, axis=1, keepdims=True), 1e-30)
+                        q = jnp.round(v * (32767.0 / top))
+                        out[(o - 1, *ind)] = q.astype(jnp.int32).astype(jnp.int16)
+                        out_scale[(o - 1, *ind)] = jnp.broadcast_to(top / 32767.0, (8, 128))
+
+                    each(others, encode)
+                    pairs = [
+                        (out.at[o - 1], got.at[o - 1]),
+                        (out_scale.at[o - 1], got_scale.at[o - 1]),
+                    ]
+                for part, (src, dst) in enumerate(pairs):
+                    copy = pltpu.make_async_remote_copy(
+                        src_ref=src,
+                        dst_ref=dst,
+                        send_sem=rs_s.at[which, axis, o - 1, part],
+                        recv_sem=rs_r.at[which, axis, o - 1, part],
+                        device_id=device(axis, peer),
+                        device_id_type=MESH,
+                    )
+                    copy.start()
+                    copies.append(copy)
             yield
             left.remove(axis)
-            own = region(left)
-            for o, copy in enumerate(copies):
+            for copy in copies:
                 copy.wait()
-            shape = [dims[a] for a in range(4) if a in left]
-
-            def total(i, carry):
-                ind, sub, rest = [], [], i
-                for a in reversed(left):
-                    ind.insert(0, lax.rem(rest, dims[a]))
-                    rest = rest // dims[a]
-                full = list(here)
-                for a, v in zip(left, ind):
-                    full[a] = v
+
+            def total(full, ind):
                 acc = buf[tuple(full)]
                 for o in range(n - 1):
-                    acc = acc + stage[(o, *ind)]
+                    v = got[(o, *ind)]
+                    if coded:
+                        v = v.astype(jnp.int32).astype(F32) * got_scale[(o, *ind)][0:1, 0:1]
+                    acc = acc + v
                 buf[tuple(full)] = acc
-                return carry
-
-            count = 1
-            for m in shape:
-                count *= m
-            if count == 1:
-                total(0, 0)
-            else:
-                lax.fori_loop(0, count, total, 0)
+
+            each(left, total)
             yield
 
     def reduce_bias():
@@ -514,11 +561,11 @@
         return carry
 
     lax.fori_loop(0, width // TILE, grad_two, 0)
-    red1 = reduce(g1, (3, 1, 2, 0), (rc1, ra1, rb1, rz1), 1)
+    red1 = reduce(g1, (3, 1, 2, 0), stages1, 1)
     next(red1)
 
     def backward(t, carry):
-        r = pl.ds(pl.multiple_of(t * TILE, TILE), TILE)
+        r = pl.ds(pl.multiple_of(t * tall, tall), tall)
         gh = lax.dot_general(
             gpb[r, :], whole(w1), (((1,), (1,)), ((), ())), preferred_element_type=F32
         )
@@ -528,7 +575,7 @@
         bsum[0:1, :] += jnp.sum(ga, 0, keepdims=True)
         return carry
 
-    lax.fori_loop(0, n_rows // TILE, backward, 0)
+    lax.fori_loop(0, n_rows // tall, backward, 0)
     bbuf[3, 0] = bsum[...]
     redb = reduce_bias()
     next(redb)
@@ -543,7 +590,7 @@
         return carry
 
     lax.fori_loop(0, width // TILE, grad_one, 0)
-    red0 = reduce(g0, (3, 2, 1, 0), (rc0, rb0, ra0, rz0), 0)
+    red0 = reduce(g0, (3, 2, 1, 0), stages0, 0)
     next(red0)
     for _ in range(2):
         next(redb, None)
@@ -552,16 +599,10 @@
         step([red1, red1])
         step([redb, redb])
 
-    def finish(layer, buf):
-        p, m, v = adam(w[layer], wm[layer], wv[layer], buf[here])
-        new_w[layer] = p
-        new_wm[layer] = m
-        new_wv[layer] = v
-
     step([red1])
-    finish(1, g1)
+    grad_out[1] = g1[here]
     step([red0])
-    finish(0, g0)
+    grad_out[0] = g0[here]
     step([redb, redb])
 
 
@@ -589,32 +630,52 @@
     blocks = cy // PW
     n_old, n_new = res_slot.shape[0], patch_cell.shape[0]
     n_rows = n_old + n_new
-    cell = ((patch_cell % blocks) * cx + patch_cell // blocks)[:, None]
-    slot = res_slot[:, None]
-    wide = jnp.tile(biases, (1, 128 // share))
-    bias8 = jnp.concatenate([jnp.zeros((1, 128), F32), wide, jnp.zeros((5, 128), F32)], 0)
+    cell = (patch_cell % blocks) * cx + patch_cell // blocks
+    ids = jnp.concatenate([res_slot, cell, trainer[:, 0]]).reshape(-1, 128)
+    ids = jnp.pad(ids, ((0, -ids.shape[0] % 8), (0, 0)))
     wire = BF16 if share % 16 == 0 else F32
     most = max(dims) - 1
     full = (*dims, share, width)
     vm = pl.BlockSpec(memory_space=pltpu.VMEM)
-    shard = jax.ShapeDtypeStruct(weights.shape, F32)
 
     def scratch(*shape, dtype=F32):
         return pltpu.VMEM(shape, dtype)
+
+    coded = share % 16 == 0
+
+    def stages(order):
+        left, found = [0, 1, 2, 3], []
+        for axis in order:
+            left.remove(axis)
+            shape = (dims[axis] - 1, *(dims[a] for a in left))
+            body = (*shape, share, width) if coded else (1,) * (len(shape) + 2)
+            scale = (*shape, 8, 128) if coded else (1,) * (len(shape) + 2)
+            kind = jnp.int16 if coded else F32
+            found.append(
+                (
+                    scratch(*body, dtype=kind),
+                    scratch(*shape, share, width, dtype=kind),
+                    scratch(*scale),
+                    scratch(*scale),
+                )
+            )
+        return tuple(found)
 
     dma = pltpu.SemaphoreType.DMA
     out = pl.pallas_call(
         functools.partial(kernel, gx_n, gy_n),
         out_shape=(
             jax.ShapeDtypeStruct(field.shape, F32),
-            shard,
-            shard,
-            shard,
+            jax.ShapeDtypeStruct(weights.shape, F32),
             jax.ShapeDtypeStruct((8, width), F32),
         ),
-        in_specs=[vm] * 6 + [pl.BlockSpec(memory_space=pl.ANY)] + [vm] * 4,
-        out_specs=[vm] * 5,
+        in_specs=[vm] * 4 + [pl.BlockSpec(memory_space=pl.ANY)] + [vm] * 2,
+        out_specs=[vm] * 3,
         scratch_shapes=[
+            scratch(n_old, 128, dtype=jnp.int32),
+            scratch(n_new, 128, dtype=jnp.int32),
+            scratch(n_new, 128, dtype=jnp.int32),
+            scratch(8, 128),
             scratch(depth + 2, cx, cy),
             scratch(depth + 2, cx, cy),
             scratch(5, depth, cx, cy),
@@ -628,7 +689,6 @@
             scratch(*dims, 8, 128),
             scratch(n_rows, width),
             scratch(n_rows, width, dtype=BF16),
-            scratch(n_rows, width, dtype=BF16),
             scratch(*full),
             scratch(*full),
             scratch(8, width),
@@ -637,22 +697,16 @@
             scratch(STEPS + 1, cx, cy),
             scratch(STEPS + 1, 2, depth, cy),
             scratch(STEPS + 1, 2, cx, cy),
-            scratch(nc - 1, nz, nx, ny, share, width),
-            scratch(nx - 1, nz, share, width),
-            scratch(ny - 1, nz, nx, share, width),
-            scratch(nz - 1, share, width),
-            scratch(nc - 1, nz, nx, ny, share, width),
-            scratch(nx - 1, nz, ny, share, width),
-            scratch(ny - 1, nz, share, width),
-            scratch(nz - 1, share, width),
+            stages((3, 2, 1, 0)),
+            stages((3, 1, 2, 0)),
             scratch(4, most + 1, 8, width),
             dma((2,)),
             dma((STEPS + 1, 4)),
             dma((STEPS + 1, 4)),
             dma((3, 4, most)),
             dma((3, 4, most)),
-            dma((2, 4, most)),
-            dma((2, 4, most)),
+            dma((2, 4, most, 2)),
+            dma((2, 4, most, 2)),
             dma((4, most)),
             dma((4, most)),
         ],
@@ -662,8 +716,9 @@
         cost_estimate=pl.CostEstimate(
             flops=10 * n_rows * width * width, bytes_accessed=32 * 2**20, transcendentals=0
         ),
-    )(field, conductivity, rate, cell, trainer, slot, reservoir, weights, w_mom, w_var, bias8)
-    state, new_w, new_wm, new_wv, bias_grad = out
+    )(field, conductivity, rate, ids, reservoir, weights, biases)
+    state, share_w, bias_grad = out
+    new_w, new_wm, new_wv = adam(weights, w_mom, w_var, share_w)
     position = lax.axis_index("gx") * gy_n + lax.axis_index("gy")
     share_b = lax.dynamic_slice_in_dim(bias_grad[:2], position * share, share, 1)
     new_b, new_bm, new_bv = adam(biases, b_mom, b_var, share_b)

time: 169 us -> 131 us (0.78)
  Pallas kernels: 153 us -> 122 us
  local copies, waits for them, and re-layouts: 12.9 us -> 3.7 us
  other arithmetic: 2.02 us -> 3.98 us
    pallas_call x1, Pallas kernels: 153 us -> 122 us  [local(): pl.pallas_call(functools.partial(kernel, gx_n, gy_n), out_shape=(jax.Shap...]
    unnamed x11 -> x13, local copies, waits for them, and re-layouts: 8.8 us -> 2.33 us
    broadcast_in_dim x3 -> x0, local copies, waits for them, and re-layouts: 2.51 us -> none  [the longest x1 1.71 us: local(): slot = res_slot[:, None]]
    sub x1 -> x2, other arithmetic: 0.66 us -> 2.58 us  [adam(): param - learn_rate * mhat / (jnp.sqrt(vhat) + tiny_eps)]
where the time goes in v3:
time: 131 us
  Pallas kernels  122 us (93%)
  other arithmetic  3.98 us (3%)
  local copies, waits for them, and re-layouts  3.7 us (3%)
    pallas_call x1, Pallas kernels, local(): pl.pallas_call(functools.partial(kernel, gx_n, gy_n), out_shape=(jax.Shap...  122 us

profile of v3, /device:TPU:0, one launch (start us, length us, event | category | flops | bytes accessed | tf_op | source)
XLA Modules:
  0.0 130.8 jit_solution(15247520557178085919)
XLA Ops:
  0.6 0.7 fusion.3
  1.3 0.7 add_bitcast_fusion
  2.0 0.6 pad.4.ids
  2.6 0.0 copy-start
  2.6 0.0 copy-start.1
  2.6 0.0 copy-start.2
  2.6 0.0 copy-start.3
  2.6 0.0 copy-start.4
  2.7 0.0 copy-start.5
  2.7 122.4 %shard_map.180 = (f32[32,64,128]{2,1,0:T(8,128)}, f32[2,32,1024]{2,1,0:T(8,128)}, f32[8,1024]{1,0:T(8,128)}) custom-call(f32[32,64,128]{2,1,0:T(8,128)} %field.1, f32[32,64,128]{2,1,0:T(8,128)} %cond.1, f32[32,64,128]{2,1,0:T(8,128)} %rate.1, s32[16,128]{1,0:T(8,128)} %pad.4.ids, bf16[2048,2048]{1,0:T(8,128)(2,1)} %store.1, f32[2,32,1024]{2,1,0:T(8,128)} %w.1, ...), custom_call_target="tpu_custom_call" | custom-call | flops 13421772800 | bytes 33554432 | tf_op jit(solution)/shard_map/pallas_call | solution.py:665
  125.1 0.0 copy-done
  125.1 0.0 copy-done.1
  125.1 0.0 copy-done.2
  125.1 1.9 %divide_subtract_fusion = (f32[2,32,1024]{2,1,0:T(8,128)}, f32[2,32,1024]{2,1,0:T(8,128)}, f32[2,32,1024]{2,1,0:T(8,128)}) fusion(f32[2,32,1024]{2,1,0:T(8,128)S(1)} %copy-done, f32[2,32,1024]{2,1,0:T(8,128)} %get-tuple-element.11, f32[2,32,1024]{2,1,0:T(8,128)S(1)} %copy-done.1, f32[2,32,1024]{2,1,0:T(8,128)S(1)} %copy-done.2), kind=kLoop, calls=%fused_computation.2 | loop fusion | flops 786432 | bytes 1835008 | tf_op jit(solution)/shard_map/sub | solution.py:31
  127.0 0.8 slice.3
  127.8 0.0 copy-done.3
  127.8 0.0 copy-done.4
  127.8 0.0 copy-done.5
  127.8 0.7 divide_subtract_fusion.1
  128.4 2.3 %copy.21 = f32[32,64,128]{2,1,0:T(8,128)} copy(f32[32,64,128]{2,1,0:T(8,128)} %get-tuple-element.26) | data formatting | bytes 2097152
Async XLA Ops:
  2.6 122.4 %copy-start = (f32[2,32,1024]{2,1,0:T(8,128)S(1)}, f32[2,32,1024]{2,1,0:T(8,128)}, u32[]{:S(2)}) copy-start(f32[2,32,1024]{2,1,0:T(8,128)} %w.1) | copy-start | bytes 786436
  2.6 122.4 %copy-start.1 = (f32[2,32,1024]{2,1,0:T(8,128)S(1)}, f32[2,32,1024]{2,1,0:T(8,128)}, u32[]{:S(2)}) copy-start(f32[2,32,1024]{2,1,0:T(8,128)} %param.21) | copy-start | bytes 786436
  2.6 122.4 %copy-start.2 = (f32[2,32,1024]{2,1,0:T(8,128)S(1)}, f32[2,32,1024]{2,1,0:T(8,128)}, u32[]{:S(2)}) copy-start(f32[2,32,1024]{2,1,0:T(8,128)} %param.22) | copy-start | bytes 786436
  2.6 125.1 %copy-start.3 = (f32[2,32]{1,0:T(2,128)S(1)}, f32[2,32]{1,0:T(2,128)}, u32[]{:S(2)}) copy-start(f32[2,32]{1,0:T(2,128)} %bias.1) | copy-start | bytes 772
  2.6 125.1 %copy-start.4 = (f32[2,32]{1,0:T(2,128)S(1)}, f32[2,32]{1,0:T(2,128)}, u32[]{:S(2)}) copy-start(f32[2,32]{1,0:T(2,128)} %param.24) | copy-start | bytes 772
  2.7 125.1 %copy-start.5 = (f32[2,32]{1,0:T(2,128)S(1)}, f32[2,32]{1,0:T(2,128)}, u32[]{:S(2)}) copy-start(f32[2,32]{1,0:T(2,128)} %param.25) | copy-start | bytes 772

commit v4 on v3

--- a/solution.py
+++ b/solution.py
@@ -74,8 +74,7 @@
     ysend,
     xrecv,
     yrecv,
-    stages0,
-    stages1,
+    stages,
     bbuf,
     half_sem,
     hs_sem,
@@ -258,18 +257,20 @@
     n_old = slot.shape[0]
     n_slots = store.shape[0]
 
+    pick_tile = 512 if n_old % 1024 == 0 else TILE
+
     def pick(col, first, last):
         def one(t, carry):
-            r = pl.ds(pl.multiple_of(t * TILE, TILE), TILE)
+            r = pl.ds(pl.multiple_of(t * pick_tile, pick_tile), pick_tile)
             hot = (
-                slot[r, 0:1] == lax.broadcasted_iota(jnp.int32, (TILE, n_slots), 1)
+                slot[r, 0:1] == lax.broadcasted_iota(jnp.int32, (pick_tile, n_slots), 1)
             ).astype(F32).astype(BF16)
             rows[r, pl.ds(col, width)] = jnp.dot(
                 hot, half[...], preferred_element_type=F32
             ).astype(BF16)
             return carry
 
-        tiles = n_old // TILE
+        tiles = n_old // pick_tile
         lax.fori_loop(tiles * first // 2, tiles * last // 2, one, 0)
 
     def shifted(u, index, z):
@@ -321,11 +322,11 @@
 
         loop(depth, one, 4)
 
+    step(gens)
+    step(gens)
     pick(0, 1, 2)
     load2 = pltpu.make_async_copy(store.at[:, pl.ds(width, width)], half, half_sem.at[1])
     load2.start()
-    step(gens)
-    step(gens)
 
     blocks = cy // PW
     per = 128 // PW
@@ -359,12 +360,14 @@
             if s == 0:
                 load2.wait()
                 pick(width, 0, 1)
+                step(gens)
+                step(gens)
             if s == 1:
                 pick(width, 1, 2)
+            if s == 2:
+                build(0, lambda z: field[z])
                 step(gens)
                 step(gens)
-            if s == 2:
-                build(0, lambda z: field[z])
             halo_wait(s + 2)
     last = bufs[STEPS % 2]
 
@@ -386,8 +389,6 @@
             hot_c, table[:, c : c + 512], preferred_element_type=F32
         ).astype(BF16)
 
-    step(gens)
-    step(gens)
     step(gens)
 
     everyone = small[...].reshape(devices, 8, 128)
@@ -441,7 +442,7 @@
         for a in left:
             count *= dims[a]
 
-        def one(i, carry):
+        def one(i):
             ind, rest = [], i
             for a in reversed(left):
                 ind.insert(0, lax.rem(rest, dims[a]))
@@ -450,28 +451,30 @@
             for a, v in zip(left, ind):
                 full[a] = v
             body(full, ind)
-            return carry
-
-        if count == 1:
-            one(0, 0)
+
+        if count <= 4:
+            for i in range(count):
+                one(i)
         else:
-            lax.fori_loop(0, count, one, 0)
-
-    def reduce(buf, order, stages, which):
+            loop(count, one, 4 if count % 4 == 0 else 1)
+
+    def reduce(buf, piece, order):
         left = [0, 1, 2, 3]
+        stage = stages[piece]
+        cols = (slice(None), pl.ds(piece % 2 * (width // 2), width // 2))
         for phase, axis in enumerate(order):
             n = dims[axis]
             others = [a for a in left if a != axis]
-            out, got, out_scale, got_scale = stages[phase]
+            out, got, out_scale, got_scale = stage[phase]
             copies = []
             for o in range(1, n):
                 peer = lax.rem(here[axis] + o, n)
-                pairs = [(buf.at[region(left, (axis, peer))], got.at[o - 1])]
+                pairs = [(buf.at[(*region(left, (axis, peer)), *cols)], got.at[o - 1])]
                 if coded:
 
                     def encode(full, ind):
                         full[axis] = peer
-                        v = buf[tuple(full)]
+                        v = buf[(*full, *cols)]
                         top = jnp.max(jnp.abs(v), axis=0, keepdims=True)
                         top = jnp.maximum(jnp.max(top, axis=1, keepdims=True), 1e-30)
                         q = jnp.round(v * (32767.0 / top))
@@ -487,8 +490,8 @@
                     copy = pltpu.make_async_remote_copy(
                         src_ref=src,
                         dst_ref=dst,
-                        send_sem=rs_s.at[which, axis, o - 1, part],
-                        recv_sem=rs_r.at[which, axis, o - 1, part],
+                        send_sem=rs_s.at[piece, axis, o - 1, part],
+                        recv_sem=rs_r.at[piece, axis, o - 1, part],
                         device_id=device(axis, peer),
                         device_id_type=MESH,
                     )
@@ -500,13 +503,13 @@
                 copy.wait()
 
             def total(full, ind):
-                acc = buf[tuple(full)]
+                acc = buf[(*full, *cols)]
                 for o in range(n - 1):
                     v = got[(o, *ind)]
                     if coded:
                         v = v.astype(jnp.int32).astype(F32) * got_scale[(o, *ind)][0:1, 0:1]
                     acc = acc + v
-                buf[tuple(full)] = acc
+                buf[(*full, *cols)] = acc
 
             each(left, total)
             yield
@@ -561,8 +564,14 @@
         return carry
 
     lax.fori_loop(0, width // TILE, grad_two, 0)
-    red1 = reduce(g1, (3, 1, 2, 0), stages1, 1)
-    next(red1)
+    layer1 = [reduce(g1, 2, (3, 1, 2, 0)), reduce(g1, 3, (3, 2, 1, 0))]
+    layer0 = [reduce(g0, 0, (3, 1, 2, 0)), reduce(g0, 1, (3, 2, 1, 0))]
+
+    def onward(pieces):
+        for piece in pieces:
+            step([piece, piece])
+
+    step(layer1)
 
     def backward(t, carry):
         r = pl.ds(pl.multiple_of(t * tall, tall), tall)
@@ -575,12 +584,13 @@
         bsum[0:1, :] += jnp.sum(ga, 0, keepdims=True)
         return carry
 
-    lax.fori_loop(0, n_rows // tall, backward, 0)
+    tiles = n_rows // tall
+    lax.fori_loop(0, tiles // 2, backward, 0)
+    onward(layer1)
+    lax.fori_loop(tiles // 2, tiles, backward, 0)
     bbuf[3, 0] = bsum[...]
     redb = reduce_bias()
     next(redb)
-    next(red1)
-    next(red1)
 
     def grad_one(j, carry):
         c = pl.ds(pl.multiple_of(j * TILE, TILE), TILE)
@@ -589,21 +599,22 @@
         )
         return carry
 
-    lax.fori_loop(0, width // TILE, grad_one, 0)
-    red0 = reduce(g0, (3, 2, 1, 0), stages0, 0)
-    next(red0)
-    for _ in range(2):
-        next(redb, None)
-    for _ in range(3):
-        step([red0, red0])
-        step([red1, red1])
-        step([redb, redb])
-
-    step([red1])
+    lax.fori_loop(0, width // TILE // 2, grad_one, 0)
+    onward(layer1)
+    onward([redb])
+    lax.fori_loop(width // TILE // 2, width // TILE, grad_one, 0)
+    step(layer0)
+    onward(layer1)
+    onward([redb])
+    onward(layer0)
+    onward([redb])
+    onward(layer0)
+    onward([redb])
+    step(layer1)
     grad_out[1] = g1[here]
-    step([red0])
+    onward(layer0)
+    step(layer0)
     grad_out[0] = g0[here]
-    step([redb, redb])
 
 
 def local(
@@ -648,13 +659,13 @@
         for axis in order:
             left.remove(axis)
             shape = (dims[axis] - 1, *(dims[a] for a in left))
-            body = (*shape, share, width) if coded else (1,) * (len(shape) + 2)
+            body = (*shape, share, width // 2) if coded else (1,) * (len(shape) + 2)
             scale = (*shape, 8, 128) if coded else (1,) * (len(shape) + 2)
             kind = jnp.int16 if coded else F32
             found.append(
                 (
                     scratch(*body, dtype=kind),
-                    scratch(*shape, share, width, dtype=kind),
+                    scratch(*shape, share, width // 2, dtype=kind),
                     scratch(*scale),
                     scratch(*scale),
                 )
@@ -697,16 +708,15 @@
             scratch(STEPS + 1, cx, cy),
             scratch(STEPS + 1, 2, depth, cy),
             scratch(STEPS + 1, 2, cx, cy),
-            stages((3, 2, 1, 0)),
-            stages((3, 1, 2, 0)),
+            tuple(stages(order) for order in ((3, 1, 2, 0), (3, 2, 1, 0)) * 2),
             scratch(4, most + 1, 8, width),
             dma((2,)),
             dma((STEPS + 1, 4)),
             dma((STEPS + 1, 4)),
             dma((3, 4, most)),
             dma((3, 4, most)),
-            dma((2, 4, most, 2)),
-            dma((2, 4, most, 2)),
+            dma((4, 4, most, 2)),
+            dma((4, 4, most, 2)),
             dma((4, most)),
             dma((4, most)),
         ],

time: 131 us -> 113 us (0.86)
  Pallas kernels: 122 us -> 105 us
    pallas_call x1, Pallas kernels: 122 us -> 105 us  [local(): pl.pallas_call(functools.partial(kernel, gx_n, gy_n), out_shape=(jax.Shap...]
where the time goes in v4:
time: 113 us
  Pallas kernels  105 us (93%)
  other arithmetic  3.98 us (4%)
  local copies, waits for them, and re-layouts  3.7 us (3%)
    pallas_call x1, Pallas kernels, local(): pl.pallas_call(functools.partial(kernel, gx_n, gy_n), out_shape=(jax.Shap...  105 us
    sub x2, other arithmetic, adam(): param - learn_rate * mhat / (jnp.sqrt(vhat) + tiny_eps)  2.58 us
    unnamed x13, local copies, waits for them, and re-layouts  2.33 us

profile of v4, /device:TPU:0, one launch (start us, length us, event | category | flops | bytes accessed | tf_op | source)
XLA Modules:
  0.0 113.0 jit_solution(13125838252264055574)
XLA Ops:
  0.6 0.7 fusion.3
  1.3 0.7 add_bitcast_fusion
  2.0 0.6 pad.4.ids
  2.6 0.0 copy-start
  2.6 0.0 copy-start.1
  2.6 0.0 copy-start.2
  2.6 0.0 copy-start.3
  2.6 0.0 copy-start.4
  2.7 0.0 copy-start.5
  2.7 104.6 %shard_map.180 = (f32[32,64,128]{2,1,0:T(8,128)}, f32[2,32,1024]{2,1,0:T(8,128)}, f32[8,1024]{1,0:T(8,128)}) custom-call(f32[32,64,128]{2,1,0:T(8,128)} %field.1, f32[32,64,128]{2,1,0:T(8,128)} %cond.1, f32[32,64,128]{2,1,0:T(8,128)} %rate.1, s32[16,128]{1,0:T(8,128)} %pad.4.ids, bf16[2048,2048]{1,0:T(8,128)(2,1)} %store.1, f32[2,32,1024]{2,1,0:T(8,128)} %w.1, ...), custom_call_target="tpu_custom_call" | custom-call | flops 13421772800 | bytes 33554432 | tf_op jit(solution)/shard_map/pallas_call | solution.py:676
  107.3 0.0 copy-done
  107.3 0.0 copy-done.1
  107.3 0.0 copy-done.2
  107.3 1.9 %divide_subtract_fusion = (f32[2,32,1024]{2,1,0:T(8,128)}, f32[2,32,1024]{2,1,0:T(8,128)}, f32[2,32,1024]{2,1,0:T(8,128)}) fusion(f32[2,32,1024]{2,1,0:T(8,128)S(1)} %copy-done, f32[2,32,1024]{2,1,0:T(8,128)} %get-tuple-element.11, f32[2,32,1024]{2,1,0:T(8,128)S(1)} %copy-done.1, f32[2,32,1024]{2,1,0:T(8,128)S(1)} %copy-done.2), kind=kLoop, calls=%fused_computation.2 | loop fusion | flops 786432 | bytes 1835008 | tf_op jit(solution)/shard_map/sub | solution.py:31
  109.2 0.8 slice.3
  110.0 0.0 copy-done.3
  110.0 0.0 copy-done.4
  110.0 0.0 copy-done.5
  110.0 0.7 divide_subtract_fusion.1
  110.7 2.3 %copy.21 = f32[32,64,128]{2,1,0:T(8,128)} copy(f32[32,64,128]{2,1,0:T(8,128)} %get-tuple-element.26) | data formatting | bytes 2097152
Async XLA Ops:
  2.6 104.6 %copy-start = (f32[2,32,1024]{2,1,0:T(8,128)S(1)}, f32[2,32,1024]{2,1,0:T(8,128)}, u32[]{:S(2)}) copy-start(f32[2,32,1024]{2,1,0:T(8,128)} %w.1) | copy-start | bytes 786436
  2.6 104.6 %copy-start.1 = (f32[2,32,1024]{2,1,0:T(8,128)S(1)}, f32[2,32,1024]{2,1,0:T(8,128)}, u32[]{:S(2)}) copy-start(f32[2,32,1024]{2,1,0:T(8,128)} %param.21) | copy-start | bytes 786436
  2.6 104.7 %copy-start.2 = (f32[2,32,1024]{2,1,0:T(8,128)S(1)}, f32[2,32,1024]{2,1,0:T(8,128)}, u32[]{:S(2)}) copy-start(f32[2,32,1024]{2,1,0:T(8,128)} %param.22) | copy-start | bytes 786436
  2.6 107.3 %copy-start.3 = (f32[2,32]{1,0:T(2,128)S(1)}, f32[2,32]{1,0:T(2,128)}, u32[]{:S(2)}) copy-start(f32[2,32]{1,0:T(2,128)} %bias.1) | copy-start | bytes 772
  2.6 107.3 %copy-start.4 = (f32[2,32]{1,0:T(2,128)S(1)}, f32[2,32]{1,0:T(2,128)}, u32[]{:S(2)}) copy-start(f32[2,32]{1,0:T(2,128)} %param.24) | copy-start | bytes 772
  2.7 107.3 %copy-start.5 = (f32[2,32]{1,0:T(2,128)S(1)}, f32[2,32]{1,0:T(2,128)}, u32[]{:S(2)}) copy-start(f32[2,32]{1,0:T(2,128)} %param.25) | copy-start | bytes 772

commit v5 on v4

--- a/solution.py
+++ b/solution.py
@@ -74,6 +74,7 @@
     ysend,
     xrecv,
     yrecv,
+    ycols,
     stages,
     bbuf,
     half_sem,
@@ -155,10 +156,8 @@
                 u = plane(z)
                 xsend[index, 0, pl.ds(z, 1), :] = u[0:1, :]
                 xsend[index, 1, pl.ds(z, 1), :] = u[cx - 1 : cx, :]
-                acc = jnp.where(lanes == z, pltpu.roll(u, z, 1), acc)
-                acc = jnp.where(
-                    lanes == depth + z, pltpu.roll(u, lax.rem(depth + z + 1, cy), 1), acc
-                )
+                ends = (lanes == 2 * z) | (lanes == lax.rem(2 * z + cy - 1, cy))
+                acc = jnp.where(ends, pltpu.roll(u, 2 * z, 1), acc)
             return acc
 
         ysend[index] = lax.fori_loop(0, depth // 8, several, jnp.zeros((cx, cy), F32))
@@ -206,6 +205,10 @@
             def _():
                 buf[index, side % 2] = zero_x if side < 2 else zero_y
 
+        ycols[...] = jnp.where(
+            lanes % 2 == 0, yrecv[index, 1], pltpu.roll(yrecv[index, 0], 2, 1)
+        )
+
     def region(done, fixed=None):
         ind = []
         for a in range(4):
@@ -278,10 +281,9 @@
         hi = xrecv[index, 1, pl.ds(z, 1), :]
         xm = jnp.where(subl == 0, lo, pltpu.roll(u, 1, 0))
         xp = jnp.where(subl == cx - 1, hi, pltpu.roll(u, cx - 1, 0))
-        left = pltpu.roll(yrecv[index, 0], lax.rem(2 * cy - depth - z, cy), 1)
-        right = pltpu.roll(yrecv[index, 1], cy - 1 - z, 1)
-        ym = jnp.where(lanes == 0, left, pltpu.roll(u, 1, 1))
-        yp = jnp.where(lanes == cy - 1, right, pltpu.roll(u, cy - 1, 1))
+        ends = pltpu.roll(ycols[...], cy - 1 - 2 * z, 1)
+        ym = jnp.where(lanes == 0, ends, pltpu.roll(u, 1, 1))
+        yp = jnp.where(lanes == cy - 1, ends, pltpu.roll(u, cy - 1, 1))
         return xm, xp, ym, yp
 
     half_step = 0.5 * time_step
@@ -320,7 +322,7 @@
                 acc = acc + coef[i, z] * un
             dst[z + 1] = acc
 
-        loop(depth, one, 4)
+        loop(depth, one, 8)
 
     step(gens)
     step(gens)
@@ -543,9 +545,9 @@
 
     across = (((0,), (0,)), ((), ()))
 
-    def store_grad(buf, col, value):
+    def store_grad(buf, col, value, start=0):
         per_tile = TILE // share
-        flat = value.reshape(per_tile, share, width)
+        flat = value.reshape(per_tile, share, value.shape[1])
 
         for i in range(per_tile):
             d = col * per_tile + i
@@ -554,6 +556,8 @@
                 lax.rem(d // (ny * nc), nx),
                 lax.rem(d // nc, ny),
                 lax.rem(d, nc),
+                :,
+                start : start + value.shape[1],
             ] = flat[i]
 
     def grad_two(j, carry):
@@ -592,18 +596,25 @@
     redb = reduce_bias()
     next(redb)
 
-    def grad_one(j, carry):
-        c = pl.ds(pl.multiple_of(j * TILE, TILE), TILE)
-        store_grad(
-            g0, j, lax.dot_general(rows[:, c], hidb[...], across, preferred_element_type=F32)
-        )
-        return carry
-
-    lax.fori_loop(0, width // TILE // 2, grad_one, 0)
-    onward(layer1)
-    onward([redb])
-    lax.fori_loop(width // TILE // 2, width // TILE, grad_one, 0)
-    step(layer0)
+    for h in range(2):
+        start = h * (width // 2)
+
+        def grad_one(j, carry):
+            c = pl.ds(pl.multiple_of(j * TILE, TILE), TILE)
+            part = lax.dot_general(
+                rows[:, c],
+                hidb[:, start : start + width // 2],
+                across,
+                preferred_element_type=F32,
+            )
+            store_grad(g0, j, part, start)
+            return carry
+
+        lax.fori_loop(0, width // TILE, grad_one, 0)
+        step([layer0[h]])
+        if h == 0:
+            onward(layer1)
+            onward([redb])
     onward(layer1)
     onward([redb])
     onward(layer0)
@@ -708,6 +719,7 @@
             scratch(STEPS + 1, cx, cy),
             scratch(STEPS + 1, 2, depth, cy),
             scratch(STEPS + 1, 2, cx, cy),
+            scratch(cx, cy),
             tuple(stages(order) for order in ((3, 1, 2, 0), (3, 2, 1, 0)) * 2),
             scratch(4, most + 1, 8, width),
             dma((2,)),

time: 113 us -> 111 us (0.982)
  Pallas kernels: 105 us -> 102 us
    pallas_call x1, Pallas kernels: 105 us -> 102 us  [local(): pl.pallas_call(functools.partial(kernel, gx_n, gy_n), out_shape=(jax.Shap...]
where the time goes in v5:
time: 111 us; the launch traced here: 110 us
  Pallas kernels  102 us (92%)
  other arithmetic  3.98 us (4%)
  local copies, waits for them, and re-layouts  3.7 us (3%)
    pallas_call x1, Pallas kernels, local(): pl.pallas_call(functools.partial(kernel, gx_n, gy_n), out_shape=(jax.Shap...  102 us
    sub x2, other arithmetic, adam(): param - learn_rate * mhat / (jnp.sqrt(vhat) + tiny_eps)  2.58 us
    unnamed x13, local copies, waits for them, and re-layouts  2.33 us

profile of v5, /device:TPU:0, one launch (start us, length us, event | category | flops | bytes accessed | tf_op | source)
XLA Modules:
  0.0 110.4 jit_solution(2691630194141079658)
XLA Ops:
  0.6 0.7 fusion.3
  1.3 0.7 add_bitcast_fusion
  2.0 0.6 pad.4.ids
  2.6 0.0 copy-start
  2.6 0.0 copy-start.1
  2.6 0.0 copy-start.2
  2.6 0.0 copy-start.3
  2.6 0.0 copy-start.4
  2.7 0.0 copy-start.5
  2.7 102.0 %shard_map.180 = (f32[32,64,128]{2,1,0:T(8,128)}, f32[2,32,1024]{2,1,0:T(8,128)}, f32[8,1024]{1,0:T(8,128)}) custom-call(f32[32,64,128]{2,1,0:T(8,128)} %field.1, f32[32,64,128]{2,1,0:T(8,128)} %cond.1, f32[32,64,128]{2,1,0:T(8,128)} %rate.1, s32[16,128]{1,0:T(8,128)} %pad.4.ids, bf16[2048,2048]{1,0:T(8,128)(2,1)} %store.1, f32[2,32,1024]{2,1,0:T(8,128)} %w.1, ...), custom_call_target="tpu_custom_call" | custom-call | flops 13421772800 | bytes 33554432 | tf_op jit(solution)/shard_map/pallas_call | solution.py:687
  104.7 0.0 copy-done
  104.7 0.0 copy-done.1
  104.7 0.0 copy-done.2
  104.8 1.9 %divide_subtract_fusion = (f32[2,32,1024]{2,1,0:T(8,128)}, f32[2,32,1024]{2,1,0:T(8,128)}, f32[2,32,1024]{2,1,0:T(8,128)}) fusion(f32[2,32,1024]{2,1,0:T(8,128)S(1)} %copy-done, f32[2,32,1024]{2,1,0:T(8,128)} %get-tuple-element.11, f32[2,32,1024]{2,1,0:T(8,128)S(1)} %copy-done.1, f32[2,32,1024]{2,1,0:T(8,128)S(1)} %copy-done.2), kind=kLoop, calls=%fused_computation.2 | loop fusion | flops 786432 | bytes 1835008 | tf_op jit(solution)/shard_map/sub | solution.py:31
  106.7 0.8 slice.3
  107.4 0.0 copy-done.3
  107.4 0.0 copy-done.4
  107.4 0.0 copy-done.5
  107.4 0.7 divide_subtract_fusion.1
  108.1 2.3 %copy.21 = f32[32,64,128]{2,1,0:T(8,128)} copy(f32[32,64,128]{2,1,0:T(8,128)} %get-tuple-element.26) | data formatting | bytes 2097152
Async XLA Ops:
  2.6 102.1 %copy-start = (f32[2,32,1024]{2,1,0:T(8,128)S(1)}, f32[2,32,1024]{2,1,0:T(8,128)}, u32[]{:S(2)}) copy-start(f32[2,32,1024]{2,1,0:T(8,128)} %w.1) | copy-start | bytes 786436
  2.6 102.1 %copy-start.1 = (f32[2,32,1024]{2,1,0:T(8,128)S(1)}, f32[2,32,1024]{2,1,0:T(8,128)}, u32[]{:S(2)}) copy-start(f32[2,32,1024]{2,1,0:T(8,128)} %param.21) | copy-start | bytes 786436
  2.6 102.1 %copy-start.2 = (f32[2,32,1024]{2,1,0:T(8,128)S(1)}, f32[2,32,1024]{2,1,0:T(8,128)}, u32[]{:S(2)}) copy-start(f32[2,32,1024]{2,1,0:T(8,128)} %param.22) | copy-start | bytes 786436
  2.6 104.8 %copy-start.3 = (f32[2,32]{1,0:T(2,128)S(1)}, f32[2,32]{1,0:T(2,128)}, u32[]{:S(2)}) copy-start(f32[2,32]{1,0:T(2,128)} %bias.1) | copy-start | bytes 772
  2.6 104.8 %copy-start.4 = (f32[2,32]{1,0:T(2,128)S(1)}, f32[2,32]{1,0:T(2,128)}, u32[]{:S(2)}) copy-start(f32[2,32]{1,0:T(2,128)} %param.24) | copy-start | bytes 772
  2.7 104.8 %copy-start.5 = (f32[2,32]{1,0:T(2,128)S(1)}, f32[2,32]{1,0:T(2,128)}, u32[]{:S(2)}) copy-start(f32[2,32]{1,0:T(2,128)} %param.25) | copy-start | bytes 772
